TPU v7x, 128 devices: a whole 4x4x4 slice. The times are simulated.
128 devices in a mesh: dp: 32 (over x, y, core), mp: 4 (over z).
Axes of the slice: x: 4, y: 4, z: 4, core: 2. Of those that a mesh axis runs over, the one named last changes fastest.
Arguments:
- layer_input: bfloat16 [32, 1024, 2304], P('dp', 'mp'), may hold values from -6 to 6
- output_grad: bfloat16 [32, 1024, 9216], P('dp', None, 'mp'), may hold values from -0.046875 to 0.046875
- error_buffer: bfloat16 [32, 2304, 9216], P('dp', None, 'mp'), may hold values from -1.5 to 1.5
- q_start: float32 [9216, 32], P('mp'), may hold values from -6 to 6
Outputs:
- error_next: bfloat16 [32, 2304, 9216], P('dp', None, 'mp')
- p_basis: float32 [2304, 32], replicated
- q_next: float32 [9216, 32], P('mp')
All inputs are finite; a program needn't handle non-finite values.
Results may differ from a plain program's by a relative error of at most 0.00045.
Values may be sent and summed in bfloat16 or wider, within the bound.
No kernel may reach another device: no remote copies, remote signals or barrier semaphores. Data moves between devices by JAX's collectives and lax.ppermute only.
A program may use at most 128 MiB of HBM per device.

v0:
```python
import jax
import jax.numpy as jnp
from jax import lax
from jax.sharding import PartitionSpec as P


def orthonormal(left, gram):
    chol = jnp.linalg.cholesky(gram)
    return lax.linalg.triangular_solve(chol, left, left_side=False, lower=True, transpose_a=True)


def local(layer_input, output_grad, error_buffer, q_start):
    highest = lax.Precision.HIGHEST
    local_grads = output_grad[0]
    gradient = lax.dot_general(
        lax.all_gather(layer_input, "mp", axis=1, tiled=True)[0],
        local_grads,
        (((0,), (0,)), ((), ())),
        preferred_element_type=jnp.float32,
    )
    combined = gradient + error_buffer[0].astype(jnp.float32)
    partial_left = jnp.dot(combined, q_start, precision=highest)
    p_sum = lax.psum(partial_left, ("dp", "mp"))
    gram = jnp.dot(p_sum.T, p_sum, precision=highest)
    p_basis = orthonormal(p_sum, gram)
    right_local = jnp.dot(combined.T, p_basis, precision=highest)
    q_next = lax.psum(right_local, "dp") / lax.axis_size("dp")
    decompressed = jnp.dot(p_basis, q_next.T, precision=highest)
    error_next = (combined - decompressed).astype(jnp.bfloat16)[None]
    return (error_next, p_basis, q_next)


def solution(mesh):
    in_specs = (P("dp", "mp", None), P("dp", None, "mp"), P("dp", None, "mp"), P("mp", None))
    out_specs = (P("dp", None, "mp"), P(), P("mp", None))
    return jax.shard_map(local, mesh=mesh, in_specs=in_specs, out_specs=out_specs, check_vma=False)
```

profile of v0, /device:TPU:1, one launch (start us, length us, event | category | flops | bytes accessed | tf_op | source)
XLA Modules:
  0.0 405.4 jit_solution(13826078973440652911)
XLA Ops:
  7.2 0.0 copy-start
  7.2 0.0 all-gather.2.cloned.1.call-start
  7.2 0.7 all-gather.2.cloned.1.call-update
  7.9 0.0 all-reduce.3.cloned.1.call-start
  8.0 57.8 %all-gather.2.cloned.1.call-done = bf16[1,1024,2304]{2,1,0:T(8,128)(2,1)} async-done(((bf16[1,256,2304]{2,1,0:T(8,128)(2,1)}), bf16[1,1024,2304]{2,1,0:T(8,128)(2,1)}) %all-gather.2.cloned.1.call-update) | async-done | bytes 4718608 | tf_op jit(solution)/shard_map/all_gather | solution.py:16
  65.8 19.9 %convert_add_fusion = f32[2304,2304]{1,0:T(8,128)} fusion(bf16[1,2304,2304]{2,1,0:T(8,128)(2,1)} %param.6, bf16[1,1024,2304]{2,1,0:T(8,128)(2,1)} %param.5, bf16[1,1024,2304]{2,1,0:T(8,128)(2,1)} %all-gather.2.cloned.1.call-done), kind=kOutput, calls=%fused_computation.1 | convolution fusion | flops 10882252800 | bytes 41287680 | tf_op jit(solution)/shard_map/dot_general | solution.py:15
  85.7 23.2 %fusion.8 = f32[2304,32]{0,1:T(8,128)} fusion(f32[2304,2304]{1,0:T(8,128)} %convert_add_fusion, f32[2304,32]{0,1:T(8,128)S(1)} %copy-done), kind=kOutput, calls=%fused_computation.17 | convolution fusion | flops 2038431744 | bytes 21823488 | tf_op jit(solution)/shard_map/dot_general | solution.py:22
  108.9 0.0 all-reduce.3.cloned.1.call-update
  108.9 0.2 all-reduce.5.cloned.1.call-start
  109.1 141.7 %all-reduce.3.cloned.1.call-done = f32[2304,32]{0,1:T(8,128)} async-done(((f32[2304,32]{0,1:T(8,128)}), f32[2304,32]{0,1:T(8,128)}) %all-reduce.3.cloned.1.call-update) | async-done | bytes 294928 | tf_op jit(solution)/shard_map/psum | solution.py:23
  250.9 1.4 fusion.9
  252.3 0.1 copy.7
  252.4 2.9 cholesky.16
  255.3 0.6 compare_reduce_fusion
  256.0 0.7 fusion.4
  256.6 2.4 custom-call.6
  259.1 1.4 fusion.5
  260.5 0.0 copy-start.1
  260.5 16.0 %fusion.10 = f32[2304,32]{0,1:T(8,128)} fusion(f32[2304,2304]{1,0:T(8,128)} %convert_add_fusion, f32[2304,32]{0,1:T(8,128)S(1)} %fusion.5), kind=kOutput, calls=%fused_computation.19 | convolution fusion | flops 2038431744 | bytes 21823488 | tf_op jit(solution)/shard_map/dot_general | solution.py:26
  276.5 0.0 all-reduce.5.cloned.1.call-update
  276.5 98.8 %all-reduce.5.cloned.1.call-done = f32[2304,32]{0,1:T(8,128)} async-done(((f32[2304,32]{0,1:T(8,128)}), f32[2304,32]{0,1:T(8,128)}) %all-reduce.5.cloned.1.call-update) | async-done | bytes 294928 | tf_op jit(solution)/shard_map/psum | solution.py:27
  375.3 1.0 broadcast_multiply_fusion
  376.3 0.0 copy-start.2
  376.3 22.5 %fusion.1 = bf16[1,2304,2304]{2,1,0:T(8,128)(2,1)} fusion(f32[2304,2304]{1,0:T(8,128)} %convert_add_fusion, f32[2304,32]{0,1:T(8,128)S(1)} %fusion.5, f32[2304,32]{0,1:T(8,128)S(1)} %broadcast_multiply_fusion), kind=kOutput, calls=%fused_computation.3 | convolution fusion | flops 2049048576 | bytes 32440320 | tf_op jit(solution)/shard_map/dot_general | solution.py:28
  (5 shorter events, 0.0 us)
Async XLA Ops:
  7.2 78.5 %copy-start = (f32[2304,32]{0,1:T(8,128)S(1)}, f32[2304,32]{0,1:T(8,128)}, u32[]{:S(2)}) copy-start(f32[2304,32]{0,1:T(8,128)} %param.7) | copy-start | bytes 884740
  7.2 58.6 %all-gather.2.cloned.1.call-start = ((), (), s32[]{:S(2)}) async-start(), calls=%async_computation | async-start | bytes 5898240 | tf_op jit(solution)/shard_map/all_gather | solution.py:16
  7.9 242.9 %all-reduce.3.cloned.1.call-start = ((), (), s32[]{:S(2)}) async-start(), calls=%async_computation.1 | async-start | bytes 589824 | tf_op jit(solution)/shard_map/psum | solution.py:23
  108.9 266.4 %all-reduce.5.cloned.1.call-start = ((), (), s32[]{:S(2)}) async-start(), calls=%async_computation.2 | async-start | bytes 589824 | tf_op jit(solution)/shard_map/psum | solution.py:27
  260.5 138.4 %copy-start.1 = (f32[2304,32]{0,1:T(8,128)}, f32[2304,32]{0,1:T(8,128)S(1)}, u32[]{:S(2)}) copy-start(f32[2304,32]{0,1:T(8,128)S(1)} %fusion.5) | copy-start | bytes 884740
  376.3 22.6 %copy-start.2 = (f32[2304,32]{0,1:T(8,128)}, f32[2304,32]{0,1:T(8,128)S(1)}, u32[]{:S(2)}) copy-start(f32[2304,32]{0,1:T(8,128)S(1)} %broadcast_multiply_fusion) | copy-start | bytes 884740
Sparse Core Ops, SparseCore 0:
  9.7 56.0 all-gather.1
  109.0 141.8 all-reduce.2
  276.7 98.5 all-reduce.4
where the time goes:
time: 406 us; the launch traced here: 405 us
  waiting for transfers between devices  299 us (74%)
  matrix products  84.5 us (21%)
  between operations  13.8 us (3%)
  other arithmetic  7.67 us (2%)
    psum x1, waiting for transfers between devices, local(): p_sum = lax.psum(partial_left, ('dp', 'mp'))  142 us
    psum x1, waiting for transfers between devices, local(): q_next = lax.psum(right_local, 'dp') / lax.axis_size('dp')  98.8 us
    all_gather x1, waiting for transfers between devices, local(): lax.all_gather(layer_input, 'mp', axis=1, tiled=True)[0]  57.8 us
    dot_general x1, matrix products, local(): partial_left = jnp.dot(combined, q_start, precision=highest)  23.2 us
    dot_general x1, matrix products, local(): decompressed = jnp.dot(p_basis, q_next.T, precision=highest)  22.5 us
    dot_general x1, matrix products, local(): lax.dot_general(lax.all_gather(layer_input, 'mp', axis=1, tiled=True)[0],...  19.9 us
    dot_general x1, matrix products, local(): right_local = jnp.dot(combined.T, p_basis, precision=highest)  16 us
  transfers between devices with their start and end apart: 3, of which 3 were waited for; matrix products, arithmetic and copies ran while one was open for 0% of the time, Pallas kernels for 0%

commit v1 on v0

v1 whole, which is shorter than its diff:
```python
import jax
import jax.numpy as jnp
from jax import lax
from jax.experimental import pallas as pl
from jax.experimental.pallas import tpu as pltpu
from jax.sharding import Mesh, PartitionSpec as P

F32, BF16 = jnp.float32, jnp.bfloat16
MIB = 1 << 20
RANK = 32
NN = (((1,), (0,)), ((), ()))
NT = (((1,), (1,)), ((), ()))


def split3(x):
    hi = x.astype(BF16)
    rest = x - hi.astype(F32)
    mid = rest.astype(BF16)
    low = (rest - mid.astype(F32)).astype(BF16)
    return hi, mid, low


def stack3(x):
    return jnp.concatenate(split3(x), axis=0)


def fold3(x):
    return (x[2 * RANK:] + x[RANK:2 * RANK]) + x[:RANK]


def dot(a, b, dims):
    return lax.dot_general(a, b, dims, preferred_element_type=F32)


def params(limit, steps=1):
    return pltpu.CompilerParams(vmem_limit_bytes=limit * MIB, dimension_semantics=("arbitrary",) * steps)


def token_product_kernel(q_ref, g_ref, t_ref, q3_ref):
    @pl.when(pl.program_id(0) == 0)
    def _():
        q3_ref[...] = stack3(q_ref[...].T)

    t_ref[0] = fold3(dot(q3_ref[...], g_ref[...], NT))


def token_product(q, grads, parts):
    tokens, cols = grads.shape
    step = tokens // parts
    return pl.pallas_call(
        token_product_kernel,
        grid=(parts,),
        in_specs=[
            pl.BlockSpec((cols, RANK), lambda i: (0, 0)),
            pl.BlockSpec((step, cols), lambda i: (i, 0)),
        ],
        out_specs=[
            pl.BlockSpec((1, RANK, step), lambda i: (i, 0, 0)),
            pl.BlockSpec((3 * RANK, cols), lambda i: (0, 0)),
        ],
        out_shape=[
            jax.ShapeDtypeStruct((parts, RANK, step), F32),
            jax.ShapeDtypeStruct((3 * RANK, cols), BF16),
        ],
        compiler_params=params(32),
        name="token_product",
    )(q, grads)


def error_product_kernel(q3_ref, e_ref, p_ref):
    p_ref[...] = fold3(dot(q3_ref[...], e_ref[...], NT))


def error_product(q3, error):
    rows, cols = error.shape
    step = 256
    return pl.pallas_call(
        error_product_kernel,
        grid=(rows // step,),
        in_specs=[
            pl.BlockSpec((3 * RANK, cols), lambda i: (0, 0)),
            pl.BlockSpec((step, cols), lambda i: (i, 0)),
        ],
        out_specs=pl.BlockSpec((RANK, step), lambda i: (0, i)),
        out_shape=jax.ShapeDtypeStruct((RANK, rows), F32),
        compiler_params=params(32),
        name="error_product",
    )(q3, error)


def cut_halves(core, full_ref, keep_ref, send_ref):
    half = RANK // 2
    wide = full_ref.shape[1] // 128
    for ref, who in ((keep_ref, core), (send_ref, 1 - core)):
        rows = full_ref[pl.ds(pl.multiple_of(who * half, half), half), :]
        for r in range(half // 8):
            for k in range(wide):
                ref[r * wide + k] = rows[8 * r:8 * r + 8, 128 * k:128 * k + 128]


def join_halves(core, mine_ref, other_ref, full_ref):
    half = RANK // 2
    wide = full_ref.shape[1] // 128
    for ref, who in ((mine_ref, core), (other_ref, 1 - core)):
        for r in range(half // 8):
            rows = pl.ds(pl.multiple_of(who * half + 8 * r, 8), 8)
            for k in range(wide):
                full_ref[rows, 128 * k:128 * k + 128] = ref[r * wide + k]


def left_kernel(core_ref, t_ref, x_ref, e_ref, keep_ref, send_ref, full_ref):
    tokens = (t_ref[0] + t_ref[1]) + (t_ref[2] + t_ref[3])
    full_ref[...] = fold3(dot(stack3(tokens), x_ref[...], NN)) + e_ref[...]
    cut_halves(core_ref[0], full_ref, keep_ref, send_ref)


def left_partial(core, tokens, inputs, error_part):
    rows = inputs.shape[1]
    tiles = RANK // 16 * rows // 128
    half = jax.ShapeDtypeStruct((tiles, 8, 128), F32)
    vmem = pl.BlockSpec(memory_space=pltpu.VMEM)
    return pl.pallas_call(
        left_kernel,
        in_specs=[pl.BlockSpec(memory_space=pltpu.SMEM), vmem, vmem, vmem],
        out_specs=[vmem, vmem],
        out_shape=[half, half],
        scratch_shapes=[pltpu.VMEM((RANK, rows), F32)],
        compiler_params=pltpu.CompilerParams(vmem_limit_bytes=32 * MIB),
        name="left_partial",
    )(core, tokens, inputs, error_part)


def right_kernel(core_ref, mine_ref, other_ref, xt_ref, g_ref, e_ref, keep_ref, send_ref, p_ref, p3_ref, xp_ref, full_ref):
    i = pl.program_id(0)
    step = g_ref.shape[1]

    @pl.when(i == 0)
    def _():
        join_halves(core_ref[0], mine_ref, other_ref, p_ref)
        p3_ref[...] = stack3(p_ref[...])
        xp_ref[...] = stack3(fold3(dot(p3_ref[...], xt_ref[...], NN)))

    part = dot(p3_ref[...], e_ref[...], NN) + dot(xp_ref[...], g_ref[...], NN)
    full_ref[:, pl.ds(pl.multiple_of(i * step, step), step)] = fold3(part)

    @pl.when(i == pl.num_programs(0) - 1)
    def _():
        cut_halves(core_ref[0], full_ref, keep_ref, send_ref)


def right_partial(core, mine, other, inputs_t, grads, error):
    rows, cols = error.shape
    tokens = grads.shape[0]
    step = 256
    tiles = RANK // 16 * cols // 128
    half = jax.ShapeDtypeStruct((tiles, 8, 128), F32)
    whole = lambda *shape: pl.BlockSpec(shape, lambda i: (0,) * len(shape))
    return pl.pallas_call(
        right_kernel,
        grid=(cols // step,),
        in_specs=[
            pl.BlockSpec(memory_space=pltpu.SMEM),
            whole(*mine.shape),
            whole(*other.shape),
            whole(rows, tokens),
            pl.BlockSpec((tokens, step), lambda i: (0, i)),
            pl.BlockSpec((rows, step), lambda i: (0, i)),
        ],
        out_specs=[whole(tiles, 8, 128), whole(tiles, 8, 128), whole(RANK, rows)],
        out_shape=[half, half, jax.ShapeDtypeStruct((RANK, rows), F32)],
        scratch_shapes=[
            pltpu.VMEM((3 * RANK, rows), BF16),
            pltpu.VMEM((3 * RANK, tokens), BF16),
            pltpu.VMEM((RANK, cols), F32),
        ],
        compiler_params=params(40),
        name="right_partial",
    )(core, mine, other, inputs_t, grads, error)


def turn_kernel(at_ref, own_ref, left_ref, right_ref, far_left_ref, far_right_ref, out_ref):
    me = at_ref[0]
    step = own_ref.shape[0]
    half = step // 2

    def put(ref, owner, offset, size):
        at = pl.multiple_of(owner * step + offset, 128)
        out_ref[:, pl.ds(at, size)] = ref[...].T

    put(own_ref, me, 0, step)
    put(left_ref, lax.rem(me + 3, 4), 0, step)
    put(right_ref, lax.rem(me + 1, 4), 0, step)
    put(far_left_ref, lax.rem(me + 2, 4), 0, half)
    put(far_right_ref, lax.rem(me + 2, 4), half, half)


def turned_inputs(at, own, left, right, far_left, far_right):
    tokens, rows = own.shape
    step = 768
    block = lambda a: pl.BlockSpec((a.shape[0], step), lambda i: (0, i))
    arrays = (own, left, right, far_left, far_right)
    return pl.pallas_call(
        turn_kernel,
        grid=(rows // step,),
        in_specs=[pl.BlockSpec(memory_space=pltpu.SMEM)] + [block(a) for a in arrays],
        out_specs=pl.BlockSpec((step, 4 * tokens), lambda i: (i, 0)),
        out_shape=jax.ShapeDtypeStruct((rows, 4 * tokens), BF16),
        compiler_params=params(32),
        name="turned_inputs",
    )(at, *arrays)


def factor_kernel(p_ref, basis_ref, u6_ref, inv_ref):
    p = p_ref[...]
    gram = lax.dot_general(p, p, NT, precision=lax.Precision.HIGHEST, preferred_element_type=F32)
    row = lax.broadcasted_iota(jnp.int32, (RANK, 1), 0)
    eye = (row == lax.broadcasted_iota(jnp.int32, (RANK, RANK), 1)).astype(F32)
    both = jnp.concatenate([gram, eye], axis=1)
    scale = jnp.zeros((RANK, 1), F32)
    for k in range(RANK):
        pivot = both[k:k + 1, k:k + 1]
        scale = jnp.where(row == k, lax.rsqrt(pivot), scale)
        factor = jnp.where(row > k, both[:, k:k + 1] / pivot, 0.0)
        both = both - factor * both[k:k + 1, :]
    inverse = both[:, RANK:] * scale
    inv_ref[...] = inverse
    u = lax.dot_general(inverse, p, NN, precision=lax.Precision.HIGHEST, preferred_element_type=F32)
    u1, u2, u3 = (term.astype(F32) for term in split3(u))
    u6 = jnp.concatenate([u1, u2, u3, u1, u2, u1, u, jnp.zeros_like(u)], axis=0).T
    basis_ref[...] = u6[:, 6 * RANK:7 * RANK]
    u6_ref[...] = u6[:, :6 * RANK].astype(BF16)


def factor(p):
    rows = p.shape[1]
    vmem = pl.BlockSpec(memory_space=pltpu.VMEM)
    return pl.pallas_call(
        factor_kernel,
        in_specs=[vmem],
        out_specs=[vmem] * 3,
        out_shape=[
            jax.ShapeDtypeStruct((rows, RANK), F32),
            jax.ShapeDtypeStruct((rows, 6 * RANK), BF16),
            jax.ShapeDtypeStruct((RANK, RANK), F32),
        ],
        compiler_params=pltpu.CompilerParams(vmem_limit_bytes=32 * MIB),
        name="factor",
    )(p)


def residual_kernel(replicas, core_ref, mine_ref, other_ref, inv_ref, u_ref, xt_ref, g_ref, e_ref, out_ref, q_ref, w6_ref, full_ref):
    @pl.when(pl.program_id(0) == 0)
    def _():
        join_halves(core_ref[0], mine_ref, other_ref, full_ref)
        w = lax.dot_general(inv_ref[...], full_ref[...], NN, precision=lax.Precision.HIGHEST, preferred_element_type=F32)
        w = w * (1.0 / replicas)
        q_ref[...] = w.T
        w1, w2, w3 = split3(-w)
        w6_ref[...] = jnp.concatenate([w1, w1, w1, w2, w2, w3], axis=0)

    total = dot(xt_ref[...], g_ref[...], NN) + dot(u_ref[...], w6_ref[...], NN)
    out_ref[0] = (total + e_ref[...].astype(F32)).astype(BF16)


def residual(core, mine, other, inverse, u6, inputs_t, grads, error, replicas):
    rows, cols = error.shape
    tokens = grads.shape[0]
    step = 256
    whole = lambda *shape: pl.BlockSpec(shape, lambda i: (0,) * len(shape))
    import functools
    return pl.pallas_call(
        functools.partial(residual_kernel, replicas),
        grid=(rows // step,),
        in_specs=[
            pl.BlockSpec(memory_space=pltpu.SMEM),
            whole(*mine.shape),
            whole(*other.shape),
            whole(RANK, RANK),
            pl.BlockSpec((step, 6 * RANK), lambda i: (i, 0)),
            pl.BlockSpec((step, tokens), lambda i: (i, 0)),
            whole(tokens, cols),
            pl.BlockSpec((step, cols), lambda i: (i, 0)),
        ],
        out_specs=[pl.BlockSpec((1, step, cols), lambda i: (0, i, 0)), whole(cols, RANK)],
        out_shape=[jax.ShapeDtypeStruct((1, rows, cols), BF16), jax.ShapeDtypeStruct((cols, RANK), F32)],
        scratch_shapes=[pltpu.VMEM((6 * RANK, cols), BF16), pltpu.VMEM((RANK, cols), F32)],
        compiler_params=params(56),
        name="residual",
    )(core, mine, other, inverse, u6, inputs_t, grads, error)


def swap(x, axis, pairs):
    return lax.ppermute(x, axis, [(a, b) for a, b in pairs] + [(b, a) for a, b in pairs])


def shift(x, by):
    return lax.ppermute(x, "z", [(i, (i + by) % 4) for i in range(4)])


def total(keep, send, over_z):
    tiles = keep.shape[0]
    places = 16
    each = -(-tiles // places)
    half = keep + swap(send, "c", [(0, 1)])
    half = jnp.pad(half, ((0, places * each - tiles), (0, 0), (0, 0)))
    parts = lax.all_to_all(half.reshape(places, each, 8, 128), ("x", "y"), 0, 0)
    part = jnp.sum(parts, axis=0)
    if over_z:
        part = part + swap(part, "z", [(0, 1), (2, 3)])
        part = part + swap(part, "z", [(1, 2), (3, 0)])
    spread = jnp.broadcast_to(part, (places,) + part.shape)
    mine = lax.all_to_all(spread, ("x", "y"), 0, 0).reshape(places * each, 8, 128)[:tiles]
    return mine, swap(mine, "c", [(0, 1)])


def local(layer_input, output_grad, error_buffer, q_start):
    inputs, grads, error = layer_input[0], output_grad[0], error_buffer[0]
    core = lax.axis_index("c").astype(jnp.int32)[None]
    at = lax.axis_index("z").astype(jnp.int32)[None]
    replicas = 32

    tokens, q3 = token_product(q_start, grads, 4)
    tokens = lax.all_to_all(tokens, "z", 0, 0)
    left = shift(inputs, 1)
    right = shift(inputs, -1)
    error_part = error_product(q3, error)
    keep, send = left_partial(core, tokens, inputs, error_part)
    half = inputs.shape[0] // 2
    far_left = shift(left[:half], 1)
    far_right = shift(right[half:], -1)
    mine, other = total(keep, send, True)
    inputs_t = turned_inputs(at, inputs, left, right, far_left, far_right)
    keep, send, p = right_partial(core, mine, other, inputs_t, grads, error)
    basis, u6, inverse = factor(p)
    mine, other = total(keep, send, False)
    error_next, q_next = residual(core, mine, other, inverse, u6, inputs_t, grads, error, replicas)
    return error_next, basis, q_next


def solution(mesh):
    fine = Mesh(mesh.devices.reshape(4, 4, 2, 4), ("x", "y", "c", "z"))
    dp = ("x", "y", "c")
    in_specs = (P(dp, "z", None), P(dp, None, "z"), P(dp, None, "z"), P("z", None))
    out_specs = (P(dp, None, "z"), P(), P("z", None))
    return jax.shard_map(local, mesh=fine, in_specs=in_specs, out_specs=out_specs, check_vma=False)
```

time: 406 us -> 150 us (0.37)
  waiting for transfers between devices: 299 us -> 16.1 us
  matrix products: 84.5 us -> 0 us
  Pallas kernels: 0 us -> 48.6 us
  blocking collectives: 0 us -> 45.4 us
  starting transfers between devices: 0.3 us -> 21.4 us
  local copies, waits for them, and re-layouts: 0.09 us -> 16.9 us
  between operations: 13.8 us -> 0.83 us
  other arithmetic: 7.67 us -> 0.08 us
    psum x2 -> x0, waiting for transfers between devices: 241 us -> none  [the longest x1 142 us: local(): p_sum = lax.psum(partial_left, ('dp', 'mp'))]
    dot_general x5 -> x0, matrix products: 83.1 us -> none  [the longest x1 23.2 us: local(): partial_left = jnp.dot(combined, q_start, precision=highest)]
    all_gather x1 -> x0, waiting for transfers between devices: 57.8 us -> none  [local(): lax.all_gather(layer_input, 'mp', axis=1, tiled=True)[0]]
    pallas_call x0 -> x7, Pallas kernels: none -> 48.6 us  [the longest x1 20.9 us: residual(): pl.pallas_call(functools.partial(residual_kernel, replicas), grid=(rows /...]
    all_to_all x0 -> x4, blocking collectives: none -> 45.4 us  [the longest x2 24 us: total(): parts = lax.all_to_all(half.reshape(places, each, 8, 128), ('x', 'y'), 0, 0)]
    ppermute x0 -> x10, starting transfers between devices: none -> 17.4 us  [the longest x6 11.3 us: swap(): lax.ppermute(x, axis, [(a, b) for a, b in pairs] + [(b, a) for a, b in pa...]
    unnamed x6 -> x23, local copies, waits for them, and re-layouts: 0.02 us -> 13.4 us
    all_to_all x0 -> x1, waiting for transfers between devices: none -> 9.66 us  [local(): tokens = lax.all_to_all(tokens, 'z', 0, 0)]
  transfers between devices with their start and end apart: 3 -> 11, of which waited for: 3 -> 4; matrix products, arithmetic and copies ran while one was open for 0% -> 4% of each run, Pallas kernels for 0% -> 11%
where the time goes in v1:
time: 150 us; the launch traced here: 149 us
  Pallas kernels  48.6 us (32%)
  blocking collectives  45.4 us (30%)
  starting transfers between devices  21.4 us (14%)
  local copies, waits for them, and re-layouts  16.9 us (11%)
  waiting for transfers between devices  16.1 us (11%)
    all_to_all x2, blocking collectives, total(): parts = lax.all_to_all(half.reshape(places, each, 8, 128), ('x', 'y'), 0, 0)  24 us
    all_to_all x2, blocking collectives, total(): lax.all_to_all(spread, ('x', 'y'), 0, 0).reshape(places * each, 8, 128)  21.4 us
    pallas_call x1, Pallas kernels, residual(): pl.pallas_call(functools.partial(residual_kernel, replicas), grid=(rows /...  20.9 us
    unnamed x23, local copies, waits for them, and re-layouts  13.4 us
    ppermute x6, starting transfers between devices, swap(): lax.ppermute(x, axis, [(a, b) for a, b in pairs] + [(b, a) for a, b in pa...  11.3 us
    pallas_call x1, Pallas kernels, right_partial(): pl.pallas_call(right_kernel, grid=(cols // step,), in_specs=[pl.BlockSpec...  10.9 us
    all_to_all x1, waiting for transfers between devices, local(): tokens = lax.all_to_all(tokens, 'z', 0, 0)  9.66 us
    ppermute x6, waiting for transfers between devices, swap(): lax.ppermute(x, axis, [(a, b) for a, b in pairs] + [(b, a) for a, b in pa...  6.43 us
  transfers between devices with their start and end apart: 11, of which 4 were waited for; matrix products, arithmetic and copies ran while one was open for 4% of the time, Pallas kernels for 11%

profile of v1, /device:TPU:1, one launch (start us, length us, event | category | flops | bytes accessed | tf_op | source)
XLA Modules:
  0.0 149.3 jit_solution(3602640252960535749)
XLA Ops:
  0.6 4.7 %collective-permute-start.5 = (bf16[256,2304]{1,0:T(8,128)(2,1)}, bf16[256,2304]{1,0:T(8,128)(2,1)S(1)}, u32[]{:S(2)}, u32[]{:S(2)}) collective-permute-start(bf16[256,2304]{1,0:T(8,128)(2,1)} %bitcast.17), channel_id=1, source_target_pairs={{0,3},{1,0},{2,1},{3,2},{4,7},{5,4},{6,5},{7,6},{8,11},{9,8},{10,9... | collective-permute-start | bytes 3538952 | tf_op jit(solution)/shard_map/ppermute | solution.py:297
  6.6 2.3 %copy-done.1 = bf16[1,1024,2304]{2,1,0:T(8,128)(2,1)S(1)} copy-done((bf16[1,1024,2304]{2,1,0:T(8,128)(2,1)S(1)}, bf16[1,1024,2304]{2,1,0:T(8,128)(2,1)}, u32[]{:S(2)}) %copy-start.1) | copy-done | bytes 4718616
  9.0 3.1 %token_product.1 = (f32[4,32,256]{2,1,0:T(8,128)}, bf16[96,2304]{1,0:T(8,128)(2,1)S(1)}) custom-call(f32[2304,32]{1,0:T(8,128)S(1)} %copy.7.q_ref, bf16[1024,2304]{1,0:T(8,128)(2,1)S(1)} %bitcast.13), custom_call_target="tpu_custom_call" | custom-call | tf_op jit(solution)/shard_map/token_product/pallas_call | solution.py:50
  12.1 3.9 %all-to-all-start = ((f32[4,32,256]{2,1,0:T(8,128)}), f32[4,32,256]{2,1,0:T(8,128)S(1)}, u32[]{:S(2)}, u32[]{:S(2)}) async-start(f32[4,32,256]{2,1,0:T(8,128)} %get-tuple-element.15), calls=%async_computation | async-start | bytes 262144 | tf_op jit(solution)/shard_map/all_to_all | solution.py:323
  16.0 4.0 %copy-done = bf16[1,2304,2304]{2,1,0:T(8,128)(2,1)S(1)} copy-done((bf16[1,2304,2304]{2,1,0:T(8,128)(2,1)S(1)}, bf16[1,2304,2304]{2,1,0:T(8,128)(2,1)}, u32[]{:S(2)}) %copy-start) | copy-done | bytes 10616856
  20.0 4.7 %error_product.1.e_ref = f32[32,2304]{1,0:T(8,128)S(1)} custom-call(bf16[96,2304]{1,0:T(8,128)(2,1)S(1)} %get-tuple-element.16.q3_ref, bf16[2304,2304]{1,0:T(8,128)(2,1)S(1)} %bitcast.11), custom_call_target="tpu_custom_call" | custom-call | tf_op jit(solution)/shard_map/error_product/pallas_call | solution.py:77
  24.7 9.7 %all-to-all-done.t_ref = f32[4,32,256]{2,1,0:T(8,128)S(1)} async-done(((f32[4,32,256]{2,1,0:T(8,128)}), f32[4,32,256]{2,1,0:T(8,128)S(1)}, u32[]{:S(2)}, u32[]{:S(2)}) %all-to-all-start) | async-done | bytes 131104 | tf_op jit(solution)/shard_map/all_to_all | solution.py:323
  34.7 2.2 %collective-permute-start = (f32[36,8,128]{2,1,0:T(8,128)S(1)}, f32[36,8,128]{2,1,0:T(8,128)S(1)}, u32[]{:S(2)}, u32[]{:S(2)}) collective-permute-start(f32[36,8,128]{2,1,0:T(8,128)S(1)} %get-tuple-element.18), channel_id=1, source_target_pairs={{0,4},{4,0},{1,5},{5,1},{2,6},{6,2},{3,7},{7,3},{8,12},{12,8},{9,1... | collective-permute-start | bytes 442376 | tf_op jit(solution)/shard_map/ppermute | solution.py:293
  37.8 1.9 %slice.25 = bf16[128,2304]{1,0:T(8,128)(2,1)} slice(bf16[256,2304]{1,0:T(8,128)(2,1)} %collective-permute-done.4.left_ref), slice={[0:128], [0:2304]} | slice | bytes 1179648 | tf_op jit(solution)/shard_map/slice | solution.py:329
  39.7 1.5 collective-permute-start.6
  41.2 13.7 %all_to_all.25 = f32[16,3,8,128]{3,2,1,0:T(8,128)S(1)} all-to-all(f32[16,3,8,128]{3,2,1,0:T(8,128)S(1)} %bitcast.21), channel_id=1, replica_groups=mesh['x'=4,'y'=4,'c'=2,'z'=4] {'x','y'}, dimensions={0} | all-to-all | bytes 393216 | tf_op jit(solution)/shard_map/all_to_all | solution.py:306
  55.1 2.5 %collective-permute-done.1 = f32[3,8,128]{2,1,0:T(8,128)S(1)} collective-permute-done((f32[3,8,128]{2,1,0:T(8,128)S(1)}, f32[3,8,128]{2,1,0:T(8,128)S(1)}, u32[]{:S(2)}, u32[]{:S(2)}) %collective-permute-start.1) | collective-permute-done | bytes 12320 | tf_op jit(solution)/shard_map/ppermute | solution.py:293
  58.8 2.5 %collective-permute-done.2 = f32[3,8,128]{2,1,0:T(8,128)S(1)} collective-permute-done((f32[3,8,128]{2,1,0:T(8,128)S(1)}, f32[3,8,128]{2,1,0:T(8,128)S(1)}, u32[]{:S(2)}, u32[]{:S(2)}) %collective-permute-start.2) | collective-permute-done | bytes 12320 | tf_op jit(solution)/shard_map/ppermute | solution.py:293
  61.4 10.8 %all_to_all.26 = f32[16,3,8,128]{3,2,1,0:T(8,128)S(1)} all-to-all(f32[16,3,8,128]{3,2,1,0:T(8,128)S(1)} %broadcast_in_dim.13), channel_id=1, replica_groups=mesh['x'=4,'y'=4,'c'=2,'z'=4] {'x','y'}, dimensions={0} | all-to-all | bytes 393216 | tf_op jit(solution)/shard_map/all_to_all | solution.py:312
  72.9 4.9 %collective-permute-start.3 = (f32[36,8,128]{2,1,0:T(8,128)}, f32[36,8,128]{2,1,0:T(8,128)}, u32[]{:S(2)}, u32[]{:S(2)}) collective-permute-start(f32[36,8,128]{2,1,0:T(8,128)} %bitcast.5.mine_ref), channel_id=1, source_target_pairs={{0,4},{4,0},{1,5},{5,1},{2,6},{6,2},{3,7},{7,3},{8,12},{12,8},{9,1... | collective-permute-start | bytes 442376 | tf_op jit(solution)/shard_map/ppermute | solution.py:293
  77.9 3.3 %turned_inputs.1.xt_ref = bf16[2304,1024]{1,0:T(8,128)(2,1)S(1)} custom-call(s32[1]{0:T(128)} %bitcast.6.at_ref, bf16[256,2304]{1,0:T(8,128)(2,1)S(1)} %bitcast.20, bf16[256,2304]{1,0:T(8,128)(2,1)} %collective-permute-done.4.left_ref, bf16[256,2304]{1,0:T(8,128)(2,1)S(1)} %collective-permute-done.5.right_ref, ...), custom_call_target="tpu_custom_call" | custom-call | tf_op jit(solution)/shard_map/turned_inputs/pallas_call | solution.py:202
  81.3 10.9 %right_partial.1 = (f32[36,8,128]{2,1,0:T(8,128)S(1)}, f32[36,8,128]{2,1,0:T(8,128)S(1)}, f32[32,2304]{1,0:T(8,128)S(1)}) custom-call(s32[1]{0:T(128)} %bitcast.core_ref, f32[36,8,128]{2,1,0:T(8,128)} %bitcast.5.mine_ref, f32[36,8,128]{2,1,0:T(8,128)} %collective-permute-done.3.other_ref, bf16[2304,1024]{1,0:T(8,128)(2,1)S(1)} %turned_inputs.1.xt_ref, ...), custom_call_target="tpu_custom_call" | custom-call | tf_op jit(solution)/shard_map/right_partial/pallas_call | solution.py:158
  92.3 1.4 collective-permute-done.8
  93.7 10.2 %all_to_all.27 = f32[16,3,8,128]{3,2,1,0:T(8,128)S(1)} all-to-all(f32[16,3,8,128]{3,2,1,0:T(8,128)S(1)} %bitcast.22), channel_id=1, replica_groups=mesh['x'=4,'y'=4,'c'=2,'z'=4] {'x','y'}, dimensions={0} | all-to-all | bytes 393216 | tf_op jit(solution)/shard_map/all_to_all | solution.py:306
  103.9 10.5 %all_to_all.28 = f32[16,3,8,128]{3,2,1,0:T(8,128)S(1)} all-to-all(f32[16,3,8,128]{3,2,1,0:T(8,128)S(1)} %broadcast_in_dim.15), channel_id=1, replica_groups=mesh['x'=4,'y'=4,'c'=2,'z'=4] {'x','y'}, dimensions={0} | all-to-all | bytes 393216 | tf_op jit(solution)/shard_map/all_to_all | solution.py:312
  114.5 2.8 %collective-permute-start.9 = (f32[36,8,128]{2,1,0:T(8,128)S(1)}, f32[36,8,128]{2,1,0:T(8,128)S(1)}, u32[]{:S(2)}, u32[]{:S(2)}) collective-permute-start(f32[36,8,128]{2,1,0:T(8,128)S(1)} %bitcast.23), channel_id=1, source_target_pairs={{0,4},{4,0},{1,5},{5,1},{2,6},{6,2},{3,7},{7,3},{8,12},{12,8},{9,1... | collective-permute-start | bytes 442376 | tf_op jit(solution)/shard_map/ppermute | solution.py:293
  117.3 5.4 %factor.1 = (f32[2304,32]{1,0:T(8,128)S(1)}, bf16[2304,192]{1,0:T(8,128)(2,1)S(1)}, f32[32,32]{1,0:T(8,128)S(1)}) custom-call(f32[32,2304]{1,0:T(8,128)S(1)} %get-tuple-element.21.p_ref), custom_call_target="tpu_custom_call" | custom-call | tf_op jit(solution)/shard_map/factor/pallas_call | solution.py:237
  126.1 20.9 %residual.1 = (bf16[1,2304,2304]{2,1,0:T(8,128)(2,1)}, f32[2304,32]{1,0:T(8,128)}) custom-call(s32[1]{0:T(128)} %bitcast.core_ref, f32[36,8,128]{2,1,0:T(8,128)} %bitcast.24, f32[36,8,128]{2,1,0:T(8,128)} %copy-done.7, f32[32,32]{1,0:T(8,128)} %copy-done.5, bf16[2304,192]{1,0:T(8,128)(2,1)} %copy-done.4, bf16[2304,1024]{1,0:T(8,128)(2,1)} %copy-done.2, ...), custom_call_target="tpu_custom_call" | custom-call | tf_op jit(solution)/shard_map/residual/pallas_call | solution.py:271
  147.0 2.3 %copy.9 = f32[2304,32]{0,1:T(8,128)} copy(f32[2304,32]{1,0:T(8,128)} %get-tuple-element.29) | data formatting | bytes 589824
  (47 shorter events, 8.2 us)
Async XLA Ops:
  0.6 36.3 %collective-permute-start.5 = (bf16[256,2304]{1,0:T(8,128)(2,1)}, bf16[256,2304]{1,0:T(8,128)(2,1)S(1)}, u32[]{:S(2)}, u32[]{:S(2)}) collective-permute-start(bf16[256,2304]{1,0:T(8,128)(2,1)} %bitcast.17), channel_id=1, source_target_pairs={{0,3},{1,0},{2,1},{3,2},{4,7},{5,4},{6,5},{7,6},{8,11},{9,8},{10,9... | collective-permute-start | bytes 3538952 | tf_op jit(solution)/shard_map/ppermute | solution.py:297
  5.3 32.5 %collective-permute-start.4 = (bf16[256,2304]{1,0:T(8,128)(2,1)}, bf16[256,2304]{1,0:T(8,128)(2,1)}, u32[]{:S(2)}, u32[]{:S(2)}) collective-permute-start(bf16[256,2304]{1,0:T(8,128)(2,1)} %bitcast.18), channel_id=1, source_target_pairs={{0,1},{1,2},{2,3},{3,0},{4,5},{5,6},{6,7},{7,4},{8,9},{9,10},{10,1... | collective-permute-start | bytes 3538952 | tf_op jit(solution)/shard_map/ppermute | solution.py:297
  6.6 2.3 %copy-start.1 = (bf16[1,1024,2304]{2,1,0:T(8,128)(2,1)S(1)}, bf16[1,1024,2304]{2,1,0:T(8,128)(2,1)}, u32[]{:S(2)}) copy-start(bf16[1,1024,2304]{2,1,0:T(8,128)(2,1)} %param.5) | copy-start | bytes 14155780
  12.1 22.3 %all-to-all-start = ((f32[4,32,256]{2,1,0:T(8,128)}), f32[4,32,256]{2,1,0:T(8,128)S(1)}, u32[]{:S(2)}, u32[]{:S(2)}) async-start(f32[4,32,256]{2,1,0:T(8,128)} %get-tuple-element.15), calls=%async_computation | async-start | bytes 262144 | tf_op jit(solution)/shard_map/all_to_all | solution.py:323
  16.0 4.0 %copy-start = (bf16[1,2304,2304]{2,1,0:T(8,128)(2,1)S(1)}, bf16[1,2304,2304]{2,1,0:T(8,128)(2,1)}, u32[]{:S(2)}) copy-start(bf16[1,2304,2304]{2,1,0:T(8,128)(2,1)} %param.6) | copy-start | bytes 31850500
  20.0 14.4 %copy-start.3 = (bf16[1,256,2304]{2,1,0:T(8,128)(2,1)S(1)}, bf16[1,256,2304]{2,1,0:T(8,128)(2,1)}, u32[]{:S(2)}) copy-start(bf16[1,256,2304]{2,1,0:T(8,128)(2,1)} %param.4) | copy-start | bytes 3538948
  34.7 6.4 %collective-permute-start = (f32[36,8,128]{2,1,0:T(8,128)S(1)}, f32[36,8,128]{2,1,0:T(8,128)S(1)}, u32[]{:S(2)}, u32[]{:S(2)}) collective-permute-start(f32[36,8,128]{2,1,0:T(8,128)S(1)} %get-tuple-element.18), channel_id=1, source_target_pairs={{0,4},{4,0},{1,5},{5,1},{2,6},{6,2},{3,7},{7,3},{8,12},{12,8},{9,1... | collective-permute-start | bytes 442376 | tf_op jit(solution)/shard_map/ppermute | solution.py:293
  37.8 40.1 %collective-permute-start.7 = (bf16[128,2304]{1,0:T(8,128)(2,1)}, bf16[128,2304]{1,0:T(8,128)(2,1)S(1)}, u32[]{:S(2)}, u32[]{:S(2)}) collective-permute-start(bf16[128,2304]{1,0:T(8,128)(2,1)} %slice.26), channel_id=1, source_target_pairs={{0,3},{1,0},{2,1},{3,2},{4,7},{5,4},{6,5},{7,6},{8,11},{9,8},{10,9... | collective-permute-start | bytes 1769480 | tf_op jit(solution)/shard_map/ppermute | solution.py:297
  39.7 38.2 %collective-permute-start.6 = (bf16[128,2304]{1,0:T(8,128)(2,1)}, bf16[128,2304]{1,0:T(8,128)(2,1)}, u32[]{:S(2)}, u32[]{:S(2)}) collective-permute-start(bf16[128,2304]{1,0:T(8,128)(2,1)} %slice.25), channel_id=1, source_target_pairs={{0,1},{1,2},{2,3},{3,0},{4,5},{5,6},{6,7},{7,4},{8,9},{9,10},{10,1... | collective-permute-start | bytes 1769480 | tf_op jit(solution)/shard_map/ppermute | solution.py:297
  55.0 2.6 %collective-permute-start.1 = (f32[3,8,128]{2,1,0:T(8,128)S(1)}, f32[3,8,128]{2,1,0:T(8,128)S(1)}, u32[]{:S(2)}, u32[]{:S(2)}) collective-permute-start(f32[3,8,128]{2,1,0:T(8,128)S(1)} %reduce_sum.18), channel_id=1, source_target_pairs={{0,1},{2,3},{1,0},{3,2},{4,5},{6,7},{5,4},{7,6},{8,9},{10,11},{9,8... | collective-permute-start | bytes 36872 | tf_op jit(solution)/shard_map/ppermute | solution.py:293
  57.6 3.8 %collective-permute-start.2 = (f32[3,8,128]{2,1,0:T(8,128)S(1)}, f32[3,8,128]{2,1,0:T(8,128)S(1)}, u32[]{:S(2)}, u32[]{:S(2)}) collective-permute-start(f32[3,8,128]{2,1,0:T(8,128)S(1)} %add.17), channel_id=1, source_target_pairs={{1,2},{3,0},{2,1},{0,3},{5,6},{7,4},{6,5},{4,7},{9,10},{11,8},{10,... | collective-permute-start | bytes 36872 | tf_op jit(solution)/shard_map/ppermute | solution.py:293
  61.4 19.8 %slice-start = ((s8[4718592]{0:T(1024)(128)(4,1)}), s8[524288]{0:T(1024)(128)(4,1)S(1)}, s32[]{:S(2)}) async-start(s8[4718592]{0:T(1024)(128)(4,1)} %bitcast.14), calls=%async_computation.5 | async-start | bytes 1048576
  72.9 8.3 %collective-permute-start.3 = (f32[36,8,128]{2,1,0:T(8,128)}, f32[36,8,128]{2,1,0:T(8,128)}, u32[]{:S(2)}, u32[]{:S(2)}) collective-permute-start(f32[36,8,128]{2,1,0:T(8,128)} %bitcast.5.mine_ref), channel_id=1, source_target_pairs={{0,4},{4,0},{1,5},{5,1},{2,6},{6,2},{3,7},{7,3},{8,12},{12,8},{9,1... | collective-permute-start | bytes 442376 | tf_op jit(solution)/shard_map/ppermute | solution.py:293
  77.9 3.4 %slice-start.1 = ((s8[4718592]{0:T(1024)(128)(4,1)}), s8[4194304]{0:T(1024)(128)(4,1)S(1)}, s32[]{:S(2)}) async-start(s8[4718592]{0:T(1024)(128)(4,1)} %bitcast.14), calls=%async_computation.6 | async-start | bytes 8388608
  81.2 10.9 %copy-start.2 = (bf16[2304,1024]{1,0:T(8,128)(2,1)}, bf16[2304,1024]{1,0:T(8,128)(2,1)S(1)}, u32[]{:S(2)}) copy-start(bf16[2304,1024]{1,0:T(8,128)(2,1)S(1)} %turned_inputs.1.xt_ref) | copy-start | bytes 14155780
  92.2 1.5 collective-permute-start.8
  114.5 10.9 %copy-start.6 = (f32[12,3,8,128]{3,2,1,0:T(8,128)}, f32[12,3,8,128]{3,2,1,0:T(8,128)S(1)}, u32[]{:S(2)}) copy-start(f32[12,3,8,128]{3,2,1,0:T(8,128)S(1)} %slice.27) | copy-start | bytes 442372
  114.5 10.9 %collective-permute-start.9 = (f32[36,8,128]{2,1,0:T(8,128)S(1)}, f32[36,8,128]{2,1,0:T(8,128)S(1)}, u32[]{:S(2)}, u32[]{:S(2)}) collective-permute-start(f32[36,8,128]{2,1,0:T(8,128)S(1)} %bitcast.23), channel_id=1, source_target_pairs={{0,4},{4,0},{1,5},{5,1},{2,6},{6,2},{3,7},{7,3},{8,12},{12,8},{9,1... | collective-permute-start | bytes 442376 | tf_op jit(solution)/shard_map/ppermute | solution.py:293
  122.7 1.1 copy-start.4
  123.8 0.6 copy-start.5
  125.4 0.7 copy-start.7

commit v2 on v0

v2 whole, which is shorter than its diff:
```python
import functools

import jax
import jax.numpy as jnp
from jax import lax
from jax.experimental import pallas as pl
from jax.experimental.pallas import tpu as pltpu
from jax.sharding import Mesh, PartitionSpec as P

F32, BF16 = jnp.float32, jnp.bfloat16
MIB = 1 << 20
RANK = 32
NN = (((1,), (0,)), ((), ()))
NT = (((1,), (1,)), ((), ()))


def split3(x):
    hi = x.astype(BF16)
    rest = x - hi.astype(F32)
    mid = rest.astype(BF16)
    low = (rest - mid.astype(F32)).astype(BF16)
    return hi, mid, low


def stack3(x):
    return jnp.concatenate(split3(x), axis=0)


def fold3(x):
    return (x[2 * RANK:] + x[RANK:2 * RANK]) + x[:RANK]


def dot(a, b, dims):
    return lax.dot_general(a, b, dims, preferred_element_type=F32)


VMEM_SPEC = pl.BlockSpec(memory_space=pltpu.VMEM)
HBM_SPEC = pl.BlockSpec(memory_space=pltpu.HBM)
SMEM_SPEC = pl.BlockSpec(memory_space=pltpu.SMEM)


def here(x):
    return pltpu.with_memory_space_constraint(x, pltpu.VMEM)


def there(x):
    return pltpu.with_memory_space_constraint(x, pltpu.HBM)


def call(kernel, name, arrays, in_specs, out_shape, out_specs, limit, scratch=(), flops=0, moved=0):
    return pl.pallas_call(
        kernel,
        in_specs=in_specs,
        out_specs=out_specs,
        out_shape=out_shape,
        scratch_shapes=list(scratch),
        compiler_params=pltpu.CompilerParams(vmem_limit_bytes=limit * MIB),
        cost_estimate=pl.CostEstimate(flops=int(flops), bytes_accessed=int(moved), transcendentals=0),
        name=name,
    )(*arrays)


def row_copy(source, target, sems, step, i):
    rows = pl.ds(pl.multiple_of(i * step, step), step)
    return pltpu.make_async_copy(source.at[rows], target.at[rows], sems.at[i])


def start_rows(source, target, sems, step):
    for i in range(source.shape[0] // step):
        row_copy(source, target, sems, step, i).start()


def for_rows(source, target, sems, step, work):
    def body(i, carry):
        row_copy(source, target, sems, step, i).wait()
        work(i)
        return carry

    lax.fori_loop(0, source.shape[0] // step, body, 0)


def turned_fold(x):
    return fold3(x.T[:3 * RANK])


def three_terms(q_t):
    terms = [term.astype(F32) for term in split3(q_t)]
    return jnp.concatenate(terms + [jnp.zeros_like(terms[0])], axis=0).T.astype(BF16)


def token_product_kernel(q_hbm, g_hbm, x_hbm, t_ref, top_ref, bottom_ref, q_ref, q3_ref, g_ref, sems, g_sems):
    step = 512
    part = t_ref.shape[2]
    half = top_ref.shape[0]
    q_copy = pltpu.make_async_copy(q_hbm, q_ref, sems.at[0])
    halves = [
        pltpu.make_async_copy(x_hbm.at[pl.ds(0, half)], top_ref, sems.at[1]),
        pltpu.make_async_copy(x_hbm.at[pl.ds(half, half)], bottom_ref, sems.at[2]),
    ]
    q_copy.start()
    start_rows(g_hbm, g_ref, g_sems, step)
    for copy in halves:
        copy.start()
    q_copy.wait()
    q3_ref[...] = three_terms(q_ref[...])

    def work(i):
        for k in range(step // part):
            rows = pl.ds(pl.multiple_of(i * step + k * part, part), part)
            t_ref[i * (step // part) + k] = turned_fold(dot(g_ref[rows, :], q3_ref[...], NN))

    for_rows(g_hbm, g_ref, g_sems, step, work)
    for copy in halves:
        copy.wait()


def token_product(q_t, grads, inputs, parts):
    tokens, cols = grads.shape
    half = inputs.shape[0] // 2
    return call(
        token_product_kernel, "token_product", (there(q_t), there(grads), there(inputs)), [HBM_SPEC] * 3,
        [
            pltpu.VMEM((parts, RANK, tokens // parts), F32),
            pltpu.VMEM((half, inputs.shape[1]), BF16),
            pltpu.VMEM((half, inputs.shape[1]), BF16),
        ],
        [VMEM_SPEC] * 3, 16,
        [
            pltpu.VMEM(q_t.shape, F32),
            pltpu.VMEM((cols, 4 * RANK), BF16),
            pltpu.VMEM((tokens, cols), BF16),
            pltpu.SemaphoreType.DMA((3,)),
            pltpu.SemaphoreType.DMA((tokens // 512,)),
        ],
        2 * 256 * tokens * cols, 2 * tokens * cols,
    )


def error_product_kernel(q_hbm, e_hbm, p_ref, q_ref, q3_ref, e_ref, sem, sems):
    step = 768
    q_copy = pltpu.make_async_copy(q_hbm, q_ref, sem)
    q_copy.start()
    start_rows(e_hbm, e_ref, sems, step)
    q_copy.wait()
    q3_ref[...] = three_terms(q_ref[...])

    def work(i):
        rows = pl.ds(pl.multiple_of(i * step, step), step)
        p_ref[:, rows] = turned_fold(dot(e_ref[rows, :], q3_ref[...], NN))

    for_rows(e_hbm, e_ref, sems, step, work)


def error_product(q_t, error):
    rows, cols = error.shape
    return call(
        error_product_kernel, "error_product", (there(q_t), there(error)), [HBM_SPEC] * 2,
        pltpu.VMEM((RANK, rows), F32), VMEM_SPEC, 16,
        [
            pltpu.VMEM(q_t.shape, F32),
            pltpu.VMEM((cols, 4 * RANK), BF16),
            pltpu.VMEM((rows, cols), BF16),
            pltpu.SemaphoreType.DMA,
            pltpu.SemaphoreType.DMA((rows // 768,)),
        ],
        10e9, 0,
    )


def cut_halves(core, full_ref, keep_ref, send_ref):
    half = RANK // 2
    wide = full_ref.shape[1] // 128
    for ref, who in ((keep_ref, core), (send_ref, 1 - core)):
        rows = full_ref[pl.ds(pl.multiple_of(who * half, half), half), :]
        for r in range(half // 8):
            for k in range(wide):
                ref[r * wide + k] = rows[8 * r:8 * r + 8, 128 * k:128 * k + 128]


def join_halves(core, mine_ref, other_ref, full_ref):
    half = RANK // 2
    wide = full_ref.shape[1] // 128
    for ref, who in ((mine_ref, core), (other_ref, 1 - core)):
        for r in range(half // 8):
            rows = pl.ds(pl.multiple_of(who * half + 8 * r, 8), 8)
            for k in range(wide):
                full_ref[rows, 128 * k:128 * k + 128] = ref[r * wide + k]


def left_kernel(core_ref, t_ref, x_ref, e_ref, keep_ref, send_ref, full_ref):
    tokens = (t_ref[0] + t_ref[1]) + (t_ref[2] + t_ref[3])
    full_ref[...] = fold3(dot(stack3(tokens), x_ref[...], NN)) + e_ref[...]
    cut_halves(core_ref[0], full_ref, keep_ref, send_ref)


def left_partial(core, tokens, inputs, error_part):
    rows = inputs.shape[1]
    half = pltpu.VMEM((RANK // 16 * rows // 128, 8, 128), F32)
    return call(
        left_kernel, "left_partial", (core, tokens, inputs, here(error_part)), [SMEM_SPEC] + [VMEM_SPEC] * 3,
        [half, half], [VMEM_SPEC] * 2, 12, [pltpu.VMEM((RANK, rows), F32)],
        2 * 256 * inputs.size, 2 * inputs.size,
    )


def right_kernel(core_ref, mine_ref, other_ref, xt_ref, g_ref, e_ref, keep_ref, send_ref, p_ref, p3_ref, xp_ref, full_ref):
    join_halves(core_ref[0], mine_ref, other_ref, p_ref)
    p3_ref[...] = stack3(p_ref[...])
    xp_ref[...] = stack3(fold3(dot(p3_ref[...], xt_ref[...], NN)))
    step = 256
    for i in range(g_ref.shape[1] // step):
        cols = slice(i * step, (i + 1) * step)
        full_ref[:, cols] = fold3(dot(p3_ref[...], e_ref[:, cols], NN) + dot(xp_ref[...], g_ref[:, cols], NN))
    cut_halves(core_ref[0], full_ref, keep_ref, send_ref)


def right_partial(core, mine, other, inputs_t, grads, error):
    rows, cols = error.shape
    tokens = grads.shape[0]
    half = pltpu.VMEM((RANK // 16 * cols // 128, 8, 128), F32)
    return call(
        right_kernel, "right_partial", (core, mine, other, here(inputs_t), here(grads), here(error)),
        [SMEM_SPEC] + [VMEM_SPEC] * 5,
        [half, half, pltpu.VMEM((RANK, rows), F32)], [VMEM_SPEC] * 3, 12,
        [
            pltpu.VMEM((3 * RANK, rows), BF16),
            pltpu.VMEM((3 * RANK, tokens), BF16),
            pltpu.VMEM((RANK, cols), F32),
        ],
        2 * 256 * (rows * cols + tokens * (rows + cols)), 0,
    )


def turn_kernel(places, at_ref, *refs):
    out_ref = refs[-1]
    tokens = out_ref.shape[1] // 4
    for (by, half), ref in zip(places, refs):
        owner = lax.rem(at_ref[0] + by, 4)
        start = pl.multiple_of(owner * tokens + half * (tokens // 2), 128)
        out_ref[:, pl.ds(start, ref.shape[0])] = ref[...].T


def turned(places, at, pieces, earlier=None, flops=0):
    rows = pieces[0].shape[1]
    arrays = tuple(pieces) if earlier is None else (*pieces, here(earlier))
    return pl.pallas_call(
        functools.partial(turn_kernel, places),
        in_specs=[SMEM_SPEC] + [VMEM_SPEC] * len(arrays),
        out_specs=VMEM_SPEC,
        out_shape=pltpu.VMEM((rows, 8 * pieces[-1].shape[0]), BF16),
        input_output_aliases={} if earlier is None else {len(arrays): 0},
        compiler_params=pltpu.CompilerParams(vmem_limit_bytes=12 * MIB),
        cost_estimate=pl.CostEstimate(flops=int(flops), bytes_accessed=0, transcendentals=0),
        name="turned",
    )(at, *arrays)


def load_kernel(g_hbm, e_hbm, g_ref, e_ref, sems):
    copies = [pltpu.make_async_copy(g_hbm, g_ref, sems.at[0]), pltpu.make_async_copy(e_hbm, e_ref, sems.at[1])]
    for copy in copies:
        copy.start()
    for copy in copies:
        copy.wait()


def loaded(grads, error):
    return call(
        load_kernel, "loaded", (there(grads), there(error)), [HBM_SPEC] * 2,
        [pltpu.VMEM(grads.shape, BF16), pltpu.VMEM(error.shape, BF16)], [VMEM_SPEC] * 2, 12,
        [pltpu.SemaphoreType.DMA((2,))], 0, 2 * (grads.size + error.size),
    )


def combined_kernel(at, rows, xt_ref, g_ref, e_ref, c_ref):
    here_rows = slice(at * rows, (at + 1) * rows)
    step = 256
    for i in range(g_ref.shape[1] // step):
        cols = slice(i * step, (i + 1) * step)
        c_ref[:, cols] = dot(xt_ref[here_rows, :], g_ref[:, cols], NN) + e_ref[here_rows, cols].astype(F32)


def combined(at, parts, inputs_t, grads, error):
    rows, cols = error.shape
    rows //= parts
    return call(
        functools.partial(combined_kernel, at, rows), "combined", (here(inputs_t), here(grads), here(error)),
        [VMEM_SPEC] * 3, pltpu.VMEM((rows, cols), F32), VMEM_SPEC, 12, (),
        2 * rows * cols * grads.shape[0], 0,
    )


def factor_kernel(p_ref, basis_ref, u6_ref, inv_ref):
    p = p_ref[...]
    gram = lax.dot_general(p, p, NT, precision=lax.Precision.HIGHEST, preferred_element_type=F32)
    row = lax.broadcasted_iota(jnp.int32, (RANK, 1), 0)
    eye = (row == lax.broadcasted_iota(jnp.int32, (RANK, RANK), 1)).astype(F32)
    both = jnp.concatenate([gram, eye], axis=1)
    scale = jnp.zeros((RANK, 1), F32)
    for k in range(RANK):
        pivot = both[k:k + 1, k:k + 1]
        scale = jnp.where(row == k, lax.rsqrt(pivot), scale)
        factor = jnp.where(row > k, both[:, k:k + 1] / pivot, 0.0)
        both = both - factor * both[k:k + 1, :]
    inverse = both[:, RANK:] * scale
    inv_ref[...] = inverse
    u = lax.dot_general(inverse, p, NN, precision=lax.Precision.HIGHEST, preferred_element_type=F32)
    u1, u2, u3 = (term.astype(F32) for term in split3(u))
    u6 = jnp.concatenate([u1, u2, u3, u1, u2, u1, u, jnp.zeros_like(u)], axis=0).T
    basis_ref[...] = u
    u6_ref[...] = u6[:, :6 * RANK].astype(BF16)


def factor(p):
    rows = p.shape[1]
    return call(
        factor_kernel, "factor", (here(p),), [VMEM_SPEC],
        [pltpu.VMEM((RANK, rows), F32), pltpu.VMEM((rows, 6 * RANK), BF16), pltpu.VMEM((RANK, RANK), F32)],
        [VMEM_SPEC] * 3, 12, (), 4e9, 0,
    )


def residual_kernel(replicas, core_ref, mine_ref, other_ref, inv_ref, u_ref, *refs):
    *c_refs, out_hbm, q_ref, full_ref, w6_ref, block_ref, sems = refs
    join_halves(core_ref[0], mine_ref, other_ref, full_ref)
    w = lax.dot_general(inv_ref[...], full_ref[...], NN, precision=lax.Precision.HIGHEST, preferred_element_type=F32)
    w = w * (1.0 / replicas)
    q_ref[...] = w
    w1, w2, w3 = split3(-w)
    w6_ref[...] = jnp.concatenate([w1, w1, w1, w2, w2, w3], axis=0)
    slots, step, width = block_ref.shape
    each = c_refs[0].shape[0] // step

    def copy_out(i):
        rows = pl.ds(pl.multiple_of(i * step, step), step)
        slot = lax.rem(i, slots)
        return pltpu.make_async_copy(block_ref.at[slot], out_hbm.at[0, rows], sems.at[slot])

    def part(s, c_ref):
        def body(k, carry):
            i = s * each + k
            slot = lax.rem(i, slots)
            rows = pl.ds(pl.multiple_of(i * step, step), step)
            c_rows = pl.ds(pl.multiple_of(k * step, step), step)

            @pl.when(i >= slots)
            def _():
                copy_out(i - slots).wait()

            for at in range(0, width, 256):
                cols = slice(at, at + 256)
                update = dot(u_ref[rows, :], w6_ref[:, cols], NN)
                block_ref[slot, :, cols] = (c_ref[c_rows, cols] + update).astype(BF16)
            copy_out(i).start()
            return carry

        lax.fori_loop(0, each, body, 0)

    for s, c_ref in enumerate(c_refs):
        part(s, c_ref)
    count = each * len(c_refs)
    for i in range(count - slots, count):
        copy_out(i).wait()


def residual(core, mine, other, inverse, u6, parts, replicas):
    cols = parts[0].shape[1]
    rows = len(parts) * parts[0].shape[0]
    step = parts[0].shape[0] // 2
    return call(
        functools.partial(residual_kernel, replicas), "residual",
        (core, mine, other, here(inverse), here(u6), *(here(part) for part in parts)),
        [SMEM_SPEC] + [VMEM_SPEC] * (4 + len(parts)),
        [pltpu.HBM((1, rows, cols), BF16), jax.ShapeDtypeStruct((RANK, cols), F32)],
        [HBM_SPEC, VMEM_SPEC], 12,
        [
            pltpu.VMEM((RANK, cols), F32),
            pltpu.VMEM((6 * RANK, cols), BF16),
            pltpu.VMEM((3, step, cols), BF16),
            pltpu.SemaphoreType.DMA((3,)),
        ],
        2 * 256 * rows * cols, 2 * rows * cols,
    )


def swap(x, axis, pairs):
    return lax.ppermute(x, axis, [(a, b) for a, b in pairs] + [(b, a) for a, b in pairs])


def shift(x, by):
    return lax.ppermute(x, "z", [(i, (i + by) % 4) for i in range(4)])


FIRST, SECOND = [(0, 1), (2, 3)], [(1, 2), (3, 0)]


def after(reason, *arrays):
    return lax.optimization_barrier((reason, *arrays))[1:]


def add_swapped(x, axis, pairs, *with_it):
    moved = swap(x, axis, pairs)
    return x + lax.optimization_barrier((moved, *with_it))[0]


def local(layer_input, output_grad, error_buffer, q_start):
    inputs, grads, error = layer_input[0], output_grad[0], error_buffer[0]
    core = lax.axis_index("c").astype(jnp.int32)[None]
    at = lax.axis_index("z").astype(jnp.int32)[None]
    replicas = 32
    tokens, top, bottom = token_product(q_start.T, grads, inputs, 4)
    (q_t,) = after(tokens, q_start.T)
    tokens = lax.all_to_all(tokens, "z", 0, 0)
    left_a, right_b = shift(top, 1), shift(bottom, -1)
    error_part = error_product(q_t, error)
    keep, send = left_partial(core, tokens, inputs, error_part)
    p = keep + swap(send, "c", [(0, 1)])
    bottom, top = after(p, bottom, top)
    left_b, right_a = shift(bottom, 1), shift(top, -1)
    p = add_swapped(p, "x", FIRST)
    inputs_t = turned(((0, 0), (3, 0), (1, 1)), at, after(p, inputs, left_a, right_b))
    p = add_swapped(p, "x", SECOND, inputs_t)
    far_a, far_b = after(p, left_a, right_b)
    far_a, far_b = shift(far_a, 1), shift(far_b, -1)
    p = add_swapped(p, "y", FIRST)
    grads, error = loaded(*after(p, grads, error))
    p = add_swapped(p, "y", SECOND, grads, error)
    left_b, right_a, inputs_t = after(p, left_b, right_a, inputs_t)
    inputs_t = turned(((3, 1), (1, 0)), at, (left_b, right_a), inputs_t, 4e9)
    p = add_swapped(p, "z", FIRST, inputs_t)
    far_a, far_b, inputs_t = after(p, far_a, far_b, inputs_t)
    inputs_t = turned(((2, 0), (2, 1)), at, (far_a, far_b), inputs_t)
    part = lambda s, reason: combined(s, 4, *after(reason, inputs_t, grads, error))
    parts = [part(0, p)]
    p = add_swapped(p, "z", SECOND, parts[0])
    keep, send, p = right_partial(core, p, swap(p, "c", [(0, 1)]), inputs_t, grads, error)

    q = keep + swap(send, "c", [(0, 1)])
    for s, (axis, pairs) in enumerate((("x", FIRST), ("x", SECOND), ("y", FIRST))):
        parts.append(part(s + 1, q))
        q = add_swapped(q, axis, pairs, parts[-1])
    basis, u6, inverse = factor(*after(q, p))
    q = add_swapped(q, "y", SECOND, basis)
    other = swap(q, "c", [(0, 1)])
    error_next, q_next = residual(core, q, other, inverse, u6, parts, replicas)
    return error_next, basis.T, q_next.T


def solution(mesh):
    fine = Mesh(mesh.devices.reshape(4, 4, 2, 4), ("x", "y", "c", "z"))
    dp = ("x", "y", "c")
    in_specs = (P(dp, "z", None), P(dp, None, "z"), P(dp, None, "z"), P("z", None))
    out_specs = (P(dp, None, "z"), P(), P("z", None))
    return jax.shard_map(local, mesh=fine, in_specs=in_specs, out_specs=out_specs, check_vma=False)
```

time: 406 us -> 104 us (0.26)
  waiting for transfers between devices: 299 us -> 16.2 us
  matrix products: 84.5 us -> 0 us
  Pallas kernels: 0 us -> 45.8 us
  starting transfers between devices: 0.3 us -> 39.6 us
  between operations: 13.8 us -> 1.03 us
  other arithmetic: 7.67 us -> 0.21 us
    psum x2 -> x0, waiting for transfers between devices: 241 us -> none  [the longest x1 142 us: local(): p_sum = lax.psum(partial_left, ('dp', 'mp'))]
    dot_general x5 -> x0, matrix products: 83.1 us -> none  [the longest x1 23.2 us: local(): partial_left = jnp.dot(combined, q_start, precision=highest)]
    all_gather x1 -> x0, waiting for transfers between devices: 57.8 us -> none  [local(): lax.all_gather(layer_input, 'mp', axis=1, tiled=True)[0]]
    pallas_call x0 -> x14, Pallas kernels: none -> 45.8 us  [the longest x11 43 us: call(): pl.pallas_call(kernel, in_specs=in_specs, out_specs=out_specs, out_shape=...]
    ppermute x0 -> x20, starting transfers between devices: none -> 33.7 us  [the longest x14 25.7 us: swap(): lax.ppermute(x, axis, [(a, b) for a, b in pairs] + [(b, a) for a, b in pa...]
    ppermute x0 -> x20, waiting for transfers between devices: none -> 16.2 us  [the longest x14 16.2 us: swap(): lax.ppermute(x, axis, [(a, b) for a, b in pairs] + [(b, a) for a, b in pa...]
    another operation x5 -> x0, other arithmetic: 6.68 us -> none  [the longest x3 3.6 us: orthonormal(): chol = jnp.linalg.cholesky(gram)]
    all_to_all x0 -> x1, starting transfers between devices: none -> 5.87 us  [local(): tokens = lax.all_to_all(tokens, 'z', 0, 0)]
  transfers between devices with their start and end apart: 3 -> 21, of which waited for: 3 -> 10; matrix products, arithmetic and copies ran while one was open for 0% -> 1% of each run, Pallas kernels for 0% -> 30%
where the time goes in v2:
time: 104 us
  Pallas kernels  45.8 us (44%)
  starting transfers between devices  39.6 us (38%)
  waiting for transfers between devices  16.2 us (16%)
    pallas_call x11, Pallas kernels, call(): pl.pallas_call(kernel, in_specs=in_specs, out_specs=out_specs, out_shape=...  43 us
    ppermute x14, starting transfers between devices, swap(): lax.ppermute(x, axis, [(a, b) for a, b in pairs] + [(b, a) for a, b in pa...  25.7 us
    ppermute x14, waiting for transfers between devices, swap(): lax.ppermute(x, axis, [(a, b) for a, b in pairs] + [(b, a) for a, b in pa...  16.2 us
    ppermute x6, starting transfers between devices, shift(): return lax.ppermute(x, 'z', [(i, (i + by) % 4) for i in range(4)])  8.06 us
    all_to_all x1, starting transfers between devices, local(): tokens = lax.all_to_all(tokens, 'z', 0, 0)  5.87 us
    pallas_call x3, Pallas kernels, turned(): pl.pallas_call(functools.partial(turn_kernel, places), in_specs=[SMEM_SPE...  2.79 us
  transfers between devices with their start and end apart: 21, of which 10 were waited for; matrix products, arithmetic and copies ran while one was open for 1% of the time, Pallas kernels for 30%

profile of v2, /device:TPU:1, one launch (start us, length us, event | category | flops | bytes accessed | tf_op | source)
XLA Modules:
  0.0 103.5 jit_solution(2758802700253322416)
XLA Ops:
  0.6 4.4 %token_product.1 = (f32[4,32,256]{2,1,0:T(8,128)}, bf16[128,2304]{1,0:T(8,128)(2,1)S(1)}, bf16[128,2304]{1,0:T(8,128)(2,1)}) custom-call(f32[32,2304]{1,0:T(8,128)} %bitcast.16, bf16[1024,2304]{1,0:T(8,128)(2,1)} %bitcast.12, bf16[256,2304]{1,0:T(8,128)(2,1)} %bitcast.9), custom_call_target="tpu_custom_call" | custom-call | flops 1207959552 | bytes 4718592 | tf_op jit(solution)/shard_map/token_product/pallas_call | solution.py:51
  5.0 5.9 %all-to-all-start = ((f32[4,32,256]{2,1,0:T(8,128)}), f32[4,32,256]{2,1,0:T(8,128)S(1)}, u32[]{:S(2)}, u32[]{:S(2)}) async-start(f32[4,32,256]{2,1,0:T(8,128)} %get-tuple-element.55), calls=%async_computation | async-start | bytes 262144 | tf_op jit(solution)/shard_map/all_to_all | solution.py:412
  10.9 1.5 %collective-permute-start.3 = (bf16[128,2304]{1,0:T(8,128)(2,1)S(1)}, bf16[128,2304]{1,0:T(8,128)(2,1)S(1)}, u32[]{:S(2)}, u32[]{:S(2)}) collective-permute-start(bf16[128,2304]{1,0:T(8,128)(2,1)S(1)} %get-tuple-element.71), channel_id=1, source_target_pairs={{0,1},{1,2},{2,3},{3,0},{4,5},{5,6},{6,7},{7,4},{8,9},{9,10},{10,1... | collective-permute-start | bytes 1769480 | tf_op jit(solution)/shard_map/ppermute | solution.py:390
  13.6 6.8 %error_product.1.e_ref = f32[32,2304]{1,0:T(8,128)S(1)} custom-call(f32[32,2304]{1,0:T(8,128)} %bitcast.17, bf16[2304,2304]{1,0:T(8,128)(2,1)} %bitcast.14), custom_call_target="tpu_custom_call" | custom-call | flops 10000000000 | tf_op jit(solution)/shard_map/error_product/pallas_call | solution.py:51
  20.8 1.6 %collective-permute-start = (f32[36,8,128]{2,1,0:T(8,128)S(1)}, f32[36,8,128]{2,1,0:T(8,128)S(1)}, u32[]{:S(2)}, u32[]{:S(2)}) collective-permute-start(f32[36,8,128]{2,1,0:T(8,128)S(1)} %get-tuple-element.58), channel_id=1, source_target_pairs={{0,4},{4,0},{1,5},{5,1},{2,6},{6,2},{3,7},{7,3},{8,12},{12,8},{9,1... | collective-permute-start | bytes 442376 | tf_op jit(solution)/shard_map/ppermute | solution.py:386
  25.3 2.2 %collective-permute-start.9 = (bf16[128,2304]{1,0:T(8,128)(2,1)S(1)}, bf16[128,2304]{1,0:T(8,128)(2,1)}, u32[]{:S(2)}, u32[]{:S(2)}) collective-permute-start(bf16[128,2304]{1,0:T(8,128)(2,1)S(1)} %get-tuple-element.71), channel_id=1, source_target_pairs={{0,3},{1,0},{2,1},{3,2},{4,7},{5,4},{6,5},{7,6},{8,11},{9,8},{10,9... | collective-permute-start | bytes 1769480 | tf_op jit(solution)/shard_map/ppermute | solution.py:390
  28.6 2.6 %collective-permute-start.2 = (f32[36,8,128]{2,1,0:T(8,128)S(1)}, f32[36,8,128]{2,1,0:T(8,128)S(1)}, u32[]{:S(2)}, u32[]{:S(2)}) collective-permute-start(f32[36,8,128]{2,1,0:T(8,128)S(1)} %add.37), channel_id=1, source_target_pairs={{32,64},{96,0},{64,32},{0,96},{33,65},{97,1},{65,33},{1,97},{34,66... | collective-permute-start | bytes 442376 | tf_op jit(solution)/shard_map/ppermute | solution.py:386
  32.0 2.4 %collective-permute-done.2 = f32[36,8,128]{2,1,0:T(8,128)S(1)} collective-permute-done((f32[36,8,128]{2,1,0:T(8,128)S(1)}, f32[36,8,128]{2,1,0:T(8,128)S(1)}, u32[]{:S(2)}, u32[]{:S(2)}) %collective-permute-start.2) | collective-permute-done | bytes 147488 | tf_op jit(solution)/shard_map/ppermute | solution.py:386
  35.8 2.6 %collective-permute-start.12 = (bf16[128,2304]{1,0:T(8,128)(2,1)S(1)}, bf16[128,2304]{1,0:T(8,128)(2,1)S(1)}, u32[]{:S(2)}, u32[]{:S(2)}) collective-permute-start(bf16[128,2304]{1,0:T(8,128)(2,1)S(1)} %collective-permute-done.4.refs_2_), channel_id=1, source_target_pairs={{0,3},{1,0},{2,1},{3,2},{4,7},{5,4},{6,5},{7,6},{8,11},{9,8},{10,9... | collective-permute-start | bytes 1769480 | tf_op jit(solution)/shard_map/ppermute | solution.py:390
  38.8 2.8 %collective-permute-start.6 = (f32[36,8,128]{2,1,0:T(8,128)S(1)}, f32[36,8,128]{2,1,0:T(8,128)S(1)}, u32[]{:S(2)}, u32[]{:S(2)}) collective-permute-start(f32[36,8,128]{2,1,0:T(8,128)S(1)} %add.39), channel_id=1, source_target_pairs={{8,16},{24,0},{16,8},{0,24},{9,17},{25,1},{17,9},{1,25},{10,18},{2... | collective-permute-start | bytes 442376 | tf_op jit(solution)/shard_map/ppermute | solution.py:386
  41.7 5.5 %loaded.1 = (bf16[1024,2304]{1,0:T(8,128)(2,1)S(1)}, bf16[2304,2304]{1,0:T(8,128)(2,1)S(1)}) custom-call(bf16[1024,2304]{1,0:T(8,128)(2,1)} %bitcast.13, bf16[2304,2304]{1,0:T(8,128)(2,1)} %bitcast.15), custom_call_target="tpu_custom_call" | custom-call | bytes 15335424 | tf_op jit(solution)/shard_map/loaded/pallas_call | solution.py:51
  47.4 1.6 %turned.4.refs_2_ = bf16[2304,1024]{1,0:T(8,128)(2,1)S(1)} custom-call(s32[1]{0:T(128)} %bitcast.5.at_ref, bf16[128,2304]{1,0:T(8,128)(2,1)} %collective-permute-done.8.refs_0_, bf16[128,2304]{1,0:T(8,128)(2,1)} %collective-permute-done.9.refs_1_, bf16[2304,1024]{1,0:T(8,128)(2,1)S(1)} %turned.3.refs_2_), custom_call_target="tpu_custom_call", output_to_operand_aliasing={{}: (3, {})} | custom-call | flops 4000000000 | tf_op jit(solution)/shard_map/turned/pallas_call | solution.py:246
  49.0 7.2 %collective-permute-done.7 = f32[36,8,128]{2,1,0:T(8,128)S(1)} collective-permute-done((f32[36,8,128]{2,1,0:T(8,128)S(1)}, f32[36,8,128]{2,1,0:T(8,128)S(1)}, u32[]{:S(2)}, u32[]{:S(2)}) %collective-permute-start.7) | collective-permute-done | bytes 147488 | tf_op jit(solution)/shard_map/ppermute | solution.py:386
  57.7 2.9 %combined.4.refs_0_ = f32[576,2304]{1,0:T(8,128)S(1)} custom-call(bf16[2304,1024]{1,0:T(8,128)(2,1)S(1)} %turned.5.xt_ref, bf16[1024,2304]{1,0:T(8,128)(2,1)S(1)} %get-tuple-element.96.g_ref, bf16[2304,2304]{1,0:T(8,128)(2,1)S(1)} %get-tuple-element.97.e_ref), custom_call_target="tpu_custom_call" | custom-call | flops 2717908992 | tf_op jit(solution)/shard_map/combined/pallas_call | solution.py:51
  61.5 2.6 %collective-permute-start.13 = (f32[36,8,128]{2,1,0:T(8,128)S(1)}, f32[36,8,128]{2,1,0:T(8,128)S(1)}, u32[]{:S(2)}, u32[]{:S(2)}) collective-permute-start(f32[36,8,128]{2,1,0:T(8,128)S(1)} %add.42.mine_ref), channel_id=1, source_target_pairs={{0,4},{4,0},{1,5},{5,1},{2,6},{6,2},{3,7},{7,3},{8,12},{12,8},{9,1... | collective-permute-start | bytes 442376 | tf_op jit(solution)/shard_map/ppermute | solution.py:386
  65.2 3.7 %right_partial.1 = (f32[36,8,128]{2,1,0:T(8,128)S(1)}, f32[36,8,128]{2,1,0:T(8,128)S(1)}, f32[32,2304]{1,0:T(8,128)S(1)}) custom-call(s32[1]{0:T(128)} %bitcast.core_ref, f32[36,8,128]{2,1,0:T(8,128)S(1)} %add.42.mine_ref, f32[36,8,128]{2,1,0:T(8,128)S(1)} %collective-permute-done.13.other_ref, bf16[2304,1024]{1,0:T(8,128)(2,1)S(1)} %turned.5.xt_ref, ...), custom_call_target="tpu_custom_call" | custom-call | flops 5133828096 | tf_op jit(solution)/shard_map/right_partial/pallas_call | solution.py:51
  71.6 2.9 %combined.5.refs_1_ = f32[576,2304]{1,0:T(8,128)S(1)} custom-call(bf16[2304,1024]{1,0:T(8,128)(2,1)S(1)} %turned.5.xt_ref, bf16[1024,2304]{1,0:T(8,128)(2,1)S(1)} %get-tuple-element.96.g_ref, bf16[2304,2304]{1,0:T(8,128)(2,1)S(1)} %get-tuple-element.97.e_ref), custom_call_target="tpu_custom_call" | custom-call | flops 2717908992 | tf_op jit(solution)/shard_map/combined/pallas_call | solution.py:51
  75.5 2.6 %collective-permute-start.16 = (f32[36,8,128]{2,1,0:T(8,128)S(1)}, f32[36,8,128]{2,1,0:T(8,128)S(1)}, u32[]{:S(2)}, u32[]{:S(2)}) collective-permute-start(f32[36,8,128]{2,1,0:T(8,128)S(1)} %add.44), channel_id=1, source_target_pairs={{32,64},{96,0},{64,32},{0,96},{33,65},{97,1},{65,33},{1,97},{34,66... | collective-permute-start | bytes 442376 | tf_op jit(solution)/shard_map/ppermute | solution.py:386
  78.0 2.9 %combined.6.refs_2_ = f32[576,2304]{1,0:T(8,128)S(1)} custom-call(bf16[2304,1024]{1,0:T(8,128)(2,1)S(1)} %turned.5.xt_ref, bf16[1024,2304]{1,0:T(8,128)(2,1)S(1)} %get-tuple-element.96.g_ref, bf16[2304,2304]{1,0:T(8,128)(2,1)S(1)} %get-tuple-element.97.e_ref), custom_call_target="tpu_custom_call" | custom-call | flops 2717908992 | tf_op jit(solution)/shard_map/combined/pallas_call | solution.py:51
  82.4 2.9 %combined.7.refs_3_ = f32[576,2304]{1,0:T(8,128)S(1)} custom-call(bf16[2304,1024]{1,0:T(8,128)(2,1)S(1)} %turned.5.xt_ref, bf16[1024,2304]{1,0:T(8,128)(2,1)S(1)} %get-tuple-element.96.g_ref, bf16[2304,2304]{1,0:T(8,128)(2,1)S(1)} %get-tuple-element.97.e_ref), custom_call_target="tpu_custom_call" | custom-call | flops 2717908992 | tf_op jit(solution)/shard_map/combined/pallas_call | solution.py:51
  85.3 2.8 %collective-permute-start.18 = (f32[36,8,128]{2,1,0:T(8,128)S(1)}, f32[36,8,128]{2,1,0:T(8,128)S(1)}, u32[]{:S(2)}, u32[]{:S(2)}) collective-permute-start(f32[36,8,128]{2,1,0:T(8,128)S(1)} %add.46), channel_id=1, source_target_pairs={{8,16},{24,0},{16,8},{0,24},{9,17},{25,1},{17,9},{1,25},{10,18},{2... | collective-permute-start | bytes 442376 | tf_op jit(solution)/shard_map/ppermute | solution.py:386
  88.1 4.1 %factor.1 = (f32[32,2304]{1,0:T(8,128)S(1)}, bf16[2304,192]{1,0:T(8,128)(2,1)S(1)}, f32[32,32]{1,0:T(8,128)S(1)}) custom-call(f32[32,2304]{1,0:T(8,128)S(1)} %get-tuple-element.100.p_ref), custom_call_target="tpu_custom_call" | custom-call | flops 4000000000 | tf_op jit(solution)/shard_map/factor/pallas_call | solution.py:51
  92.3 3.6 %collective-permute-start.19 = (f32[36,8,128]{2,1,0:T(8,128)S(1)}, f32[36,8,128]{2,1,0:T(8,128)S(1)}, u32[]{:S(2)}, u32[]{:S(2)}) collective-permute-start(f32[36,8,128]{2,1,0:T(8,128)S(1)} %add.47.mine_ref), channel_id=1, source_target_pairs={{0,4},{4,0},{1,5},{5,1},{2,6},{6,2},{3,7},{7,3},{8,12},{12,8},{9,1... | collective-permute-start | bytes 442376 | tf_op jit(solution)/shard_map/ppermute | solution.py:386
  96.9 6.4 %residual.1 = (bf16[1,2304,2304]{2,1,0:T(8,128)(2,1)}, f32[32,2304]{1,0:T(8,128)}) custom-call(s32[1]{0:T(128)} %bitcast.core_ref, f32[36,8,128]{2,1,0:T(8,128)S(1)} %add.47.mine_ref, f32[36,8,128]{2,1,0:T(8,128)S(1)} %collective-permute-done.19.other_ref, f32[32,32]{1,0:T(8,128)S(1)} %get-tuple-element.103.inv_ref, ...), custom_call_target="tpu_custom_call" | custom-call | flops 2717908992 | bytes 10616832 | tf_op jit(solution)/shard_map/residual/pallas_call | solution.py:51
  (47 shorter events, 18.0 us)
Async XLA Ops:
  5.0 15.4 %all-to-all-start = ((f32[4,32,256]{2,1,0:T(8,128)}), f32[4,32,256]{2,1,0:T(8,128)S(1)}, u32[]{:S(2)}, u32[]{:S(2)}) async-start(f32[4,32,256]{2,1,0:T(8,128)} %get-tuple-element.55), calls=%async_computation | async-start | bytes 262144 | tf_op jit(solution)/shard_map/all_to_all | solution.py:412
  10.9 20.3 %collective-permute-start.3 = (bf16[128,2304]{1,0:T(8,128)(2,1)S(1)}, bf16[128,2304]{1,0:T(8,128)(2,1)S(1)}, u32[]{:S(2)}, u32[]{:S(2)}) collective-permute-start(bf16[128,2304]{1,0:T(8,128)(2,1)S(1)} %get-tuple-element.71), channel_id=1, source_target_pairs={{0,1},{1,2},{2,3},{3,0},{4,5},{5,6},{6,7},{7,4},{8,9},{9,10},{10,1... | collective-permute-start | bytes 1769480 | tf_op jit(solution)/shard_map/ppermute | solution.py:390
  12.4 18.8 %collective-permute-start.4 = (bf16[128,2304]{1,0:T(8,128)(2,1)}, bf16[128,2304]{1,0:T(8,128)(2,1)S(1)}, u32[]{:S(2)}, u32[]{:S(2)}) collective-permute-start(bf16[128,2304]{1,0:T(8,128)(2,1)} %get-tuple-element.70), channel_id=1, source_target_pairs={{0,3},{1,0},{2,1},{3,2},{4,7},{5,4},{6,5},{7,6},{8,11},{9,8},{10,9... | collective-permute-start | bytes 1769480 | tf_op jit(solution)/shard_map/ppermute | solution.py:390
  13.6 6.9 %copy-start = (bf16[1,256,2304]{2,1,0:T(8,128)(2,1)S(1)}, bf16[1,256,2304]{2,1,0:T(8,128)(2,1)}, u32[]{:S(2)}) copy-start(bf16[1,256,2304]{2,1,0:T(8,128)(2,1)} %param.4) | copy-start | bytes 3538948
  20.8 2.6 %collective-permute-start = (f32[36,8,128]{2,1,0:T(8,128)S(1)}, f32[36,8,128]{2,1,0:T(8,128)S(1)}, u32[]{:S(2)}, u32[]{:S(2)}) collective-permute-start(f32[36,8,128]{2,1,0:T(8,128)S(1)} %get-tuple-element.58), channel_id=1, source_target_pairs={{0,4},{4,0},{1,5},{5,1},{2,6},{6,2},{3,7},{7,3},{8,12},{12,8},{9,1... | collective-permute-start | bytes 442376 | tf_op jit(solution)/shard_map/ppermute | solution.py:386
  23.5 5.1 %collective-permute-start.1 = (f32[36,8,128]{2,1,0:T(8,128)S(1)}, f32[36,8,128]{2,1,0:T(8,128)S(1)}, u32[]{:S(2)}, u32[]{:S(2)}) collective-permute-start(f32[36,8,128]{2,1,0:T(8,128)S(1)} %add.36), channel_id=1, source_target_pairs={{0,32},{64,96},{32,0},{96,64},{1,33},{65,97},{33,1},{97,65},{2,34}... | collective-permute-start | bytes 442376 | tf_op jit(solution)/shard_map/ppermute | solution.py:386
  24.8 22.6 %collective-permute-start.8 = (bf16[128,2304]{1,0:T(8,128)(2,1)}, bf16[128,2304]{1,0:T(8,128)(2,1)}, u32[]{:S(2)}, u32[]{:S(2)}) collective-permute-start(bf16[128,2304]{1,0:T(8,128)(2,1)} %get-tuple-element.70), channel_id=1, source_target_pairs={{0,1},{1,2},{2,3},{3,0},{4,5},{5,6},{6,7},{7,4},{8,9},{9,10},{10,1... | collective-permute-start | bytes 1769480 | tf_op jit(solution)/shard_map/ppermute | solution.py:390
  25.3 22.1 %collective-permute-start.9 = (bf16[128,2304]{1,0:T(8,128)(2,1)S(1)}, bf16[128,2304]{1,0:T(8,128)(2,1)}, u32[]{:S(2)}, u32[]{:S(2)}) collective-permute-start(bf16[128,2304]{1,0:T(8,128)(2,1)S(1)} %get-tuple-element.71), channel_id=1, source_target_pairs={{0,3},{1,0},{2,1},{3,2},{4,7},{5,4},{6,5},{7,6},{8,11},{9,8},{10,9... | collective-permute-start | bytes 1769480 | tf_op jit(solution)/shard_map/ppermute | solution.py:390
  28.6 5.7 %collective-permute-start.2 = (f32[36,8,128]{2,1,0:T(8,128)S(1)}, f32[36,8,128]{2,1,0:T(8,128)S(1)}, u32[]{:S(2)}, u32[]{:S(2)}) collective-permute-start(f32[36,8,128]{2,1,0:T(8,128)S(1)} %add.37), channel_id=1, source_target_pairs={{32,64},{96,0},{64,32},{0,96},{33,65},{97,1},{65,33},{1,97},{34,66... | collective-permute-start | bytes 442376 | tf_op jit(solution)/shard_map/ppermute | solution.py:386
  34.3 4.5 %collective-permute-start.5 = (f32[36,8,128]{2,1,0:T(8,128)S(1)}, f32[36,8,128]{2,1,0:T(8,128)S(1)}, u32[]{:S(2)}, u32[]{:S(2)}) collective-permute-start(f32[36,8,128]{2,1,0:T(8,128)S(1)} %add.38), channel_id=1, source_target_pairs={{0,8},{16,24},{8,0},{24,16},{1,9},{17,25},{9,1},{25,17},{2,10},{18... | collective-permute-start | bytes 442376 | tf_op jit(solution)/shard_map/ppermute | solution.py:386
  35.7 21.6 %collective-permute-start.11 = (bf16[128,2304]{1,0:T(8,128)(2,1)S(1)}, bf16[128,2304]{1,0:T(8,128)(2,1)S(1)}, u32[]{:S(2)}, u32[]{:S(2)}) collective-permute-start(bf16[128,2304]{1,0:T(8,128)(2,1)S(1)} %collective-permute-done.3.refs_1_), channel_id=1, source_target_pairs={{0,1},{1,2},{2,3},{3,0},{4,5},{5,6},{6,7},{7,4},{8,9},{9,10},{10,1... | collective-permute-start | bytes 1769480 | tf_op jit(solution)/shard_map/ppermute | solution.py:390
  35.8 21.5 %collective-permute-start.12 = (bf16[128,2304]{1,0:T(8,128)(2,1)S(1)}, bf16[128,2304]{1,0:T(8,128)(2,1)S(1)}, u32[]{:S(2)}, u32[]{:S(2)}) collective-permute-start(bf16[128,2304]{1,0:T(8,128)(2,1)S(1)} %collective-permute-done.4.refs_2_), channel_id=1, source_target_pairs={{0,3},{1,0},{2,1},{3,2},{4,7},{5,4},{6,5},{7,6},{8,11},{9,8},{10,9... | collective-permute-start | bytes 1769480 | tf_op jit(solution)/shard_map/ppermute | solution.py:390
  38.8 8.3 %collective-permute-start.6 = (f32[36,8,128]{2,1,0:T(8,128)S(1)}, f32[36,8,128]{2,1,0:T(8,128)S(1)}, u32[]{:S(2)}, u32[]{:S(2)}) collective-permute-start(f32[36,8,128]{2,1,0:T(8,128)S(1)} %add.39), channel_id=1, source_target_pairs={{8,16},{24,0},{16,8},{0,24},{9,17},{25,1},{17,9},{1,25},{10,18},{2... | collective-permute-start | bytes 442376 | tf_op jit(solution)/shard_map/ppermute | solution.py:386
  47.2 9.0 %collective-permute-start.7 = (f32[36,8,128]{2,1,0:T(8,128)S(1)}, f32[36,8,128]{2,1,0:T(8,128)S(1)}, u32[]{:S(2)}, u32[]{:S(2)}) collective-permute-start(f32[36,8,128]{2,1,0:T(8,128)S(1)} %add.40), channel_id=1, source_target_pairs={{0,1},{2,3},{1,0},{3,2},{4,5},{6,7},{5,4},{7,6},{8,9},{10,11},{9,8... | collective-permute-start | bytes 442376 | tf_op jit(solution)/shard_map/ppermute | solution.py:386
  56.2 5.3 %collective-permute-start.10 = (f32[36,8,128]{2,1,0:T(8,128)S(1)}, f32[36,8,128]{2,1,0:T(8,128)S(1)}, u32[]{:S(2)}, u32[]{:S(2)}) collective-permute-start(f32[36,8,128]{2,1,0:T(8,128)S(1)} %add.41), channel_id=1, source_target_pairs={{1,2},{3,0},{2,1},{0,3},{5,6},{7,4},{6,5},{4,7},{9,10},{11,8},{10,... | collective-permute-start | bytes 442376 | tf_op jit(solution)/shard_map/ppermute | solution.py:386
  61.5 3.6 %collective-permute-start.13 = (f32[36,8,128]{2,1,0:T(8,128)S(1)}, f32[36,8,128]{2,1,0:T(8,128)S(1)}, u32[]{:S(2)}, u32[]{:S(2)}) collective-permute-start(f32[36,8,128]{2,1,0:T(8,128)S(1)} %add.42.mine_ref), channel_id=1, source_target_pairs={{0,4},{4,0},{1,5},{5,1},{2,6},{6,2},{3,7},{7,3},{8,12},{12,8},{9,1... | collective-permute-start | bytes 442376 | tf_op jit(solution)/shard_map/ppermute | solution.py:386
  68.8 1.5 %collective-permute-start.14 = (f32[36,8,128]{2,1,0:T(8,128)S(1)}, f32[36,8,128]{2,1,0:T(8,128)S(1)}, u32[]{:S(2)}, u32[]{:S(2)}) collective-permute-start(f32[36,8,128]{2,1,0:T(8,128)S(1)} %get-tuple-element.86), channel_id=1, source_target_pairs={{0,4},{4,0},{1,5},{5,1},{2,6},{6,2},{3,7},{7,3},{8,12},{12,8},{9,1... | collective-permute-start | bytes 442376 | tf_op jit(solution)/shard_map/ppermute | solution.py:386
  70.3 5.1 %collective-permute-start.15 = (f32[36,8,128]{2,1,0:T(8,128)S(1)}, f32[36,8,128]{2,1,0:T(8,128)S(1)}, u32[]{:S(2)}, u32[]{:S(2)}) collective-permute-start(f32[36,8,128]{2,1,0:T(8,128)S(1)} %add.43), channel_id=1, source_target_pairs={{0,32},{64,96},{32,0},{96,64},{1,33},{65,97},{33,1},{97,65},{2,34}... | collective-permute-start | bytes 442376 | tf_op jit(solution)/shard_map/ppermute | solution.py:386
  75.5 5.5 %collective-permute-start.16 = (f32[36,8,128]{2,1,0:T(8,128)S(1)}, f32[36,8,128]{2,1,0:T(8,128)S(1)}, u32[]{:S(2)}, u32[]{:S(2)}) collective-permute-start(f32[36,8,128]{2,1,0:T(8,128)S(1)} %add.44), channel_id=1, source_target_pairs={{32,64},{96,0},{64,32},{0,96},{33,65},{97,1},{65,33},{1,97},{34,66... | collective-permute-start | bytes 442376 | tf_op jit(solution)/shard_map/ppermute | solution.py:386
  81.0 4.3 %collective-permute-start.17 = (f32[36,8,128]{2,1,0:T(8,128)S(1)}, f32[36,8,128]{2,1,0:T(8,128)S(1)}, u32[]{:S(2)}, u32[]{:S(2)}) collective-permute-start(f32[36,8,128]{2,1,0:T(8,128)S(1)} %add.45), channel_id=1, source_target_pairs={{0,8},{16,24},{8,0},{24,16},{1,9},{17,25},{9,1},{25,17},{2,10},{18... | collective-permute-start | bytes 442376 | tf_op jit(solution)/shard_map/ppermute | solution.py:386
  85.3 6.9 %collective-permute-start.18 = (f32[36,8,128]{2,1,0:T(8,128)S(1)}, f32[36,8,128]{2,1,0:T(8,128)S(1)}, u32[]{:S(2)}, u32[]{:S(2)}) collective-permute-start(f32[36,8,128]{2,1,0:T(8,128)S(1)} %add.46), channel_id=1, source_target_pairs={{8,16},{24,0},{16,8},{0,24},{9,17},{25,1},{17,9},{1,25},{10,18},{2... | collective-permute-start | bytes 442376 | tf_op jit(solution)/shard_map/ppermute | solution.py:386
  92.3 4.6 %collective-permute-start.19 = (f32[36,8,128]{2,1,0:T(8,128)S(1)}, f32[36,8,128]{2,1,0:T(8,128)S(1)}, u32[]{:S(2)}, u32[]{:S(2)}) collective-permute-start(f32[36,8,128]{2,1,0:T(8,128)S(1)} %add.47.mine_ref), channel_id=1, source_target_pairs={{0,4},{4,0},{1,5},{5,1},{2,6},{6,2},{3,7},{7,3},{8,12},{12,8},{9,1... | collective-permute-start | bytes 442376 | tf_op jit(solution)/shard_map/ppermute | solution.py:386

commit v3 on v2

--- a/solution.py
+++ b/solution.py
@@ -88,7 +88,7 @@
     return jnp.concatenate(terms + [jnp.zeros_like(terms[0])], axis=0).T.astype(BF16)
 
 
-def token_product_kernel(q_hbm, g_hbm, x_hbm, t_ref, top_ref, bottom_ref, q_ref, q3_ref, g_ref, sems, g_sems):
+def token_product_kernel(core_ref, q_hbm, g_hbm, x_hbm, t_ref, top_ref, bottom_ref, q_ref, q3_ref, g_ref, sems, g_sems):
     step = 512
     part = t_ref.shape[2]
     half = top_ref.shape[0]
@@ -101,8 +101,11 @@
     start_rows(g_hbm, g_ref, g_sems, step)
     for copy in halves:
         copy.start()
-    q_copy.wait()
-    q3_ref[...] = three_terms(q_ref[...])
+
+    @pl.when(core_ref[0] >= 0)
+    def _():
+        q_copy.wait()
+        q3_ref[...] = three_terms(q_ref[...])
 
     def work(i):
         for k in range(step // part):
@@ -114,11 +117,11 @@
         copy.wait()
 
 
-def token_product(q_t, grads, inputs, parts):
+def token_product(core, q_t, grads, inputs, parts):
     tokens, cols = grads.shape
     half = inputs.shape[0] // 2
     return call(
-        token_product_kernel, "token_product", (there(q_t), there(grads), there(inputs)), [HBM_SPEC] * 3,
+        token_product_kernel, "token_product", (core, there(q_t), there(grads), there(inputs)), [SMEM_SPEC] + [HBM_SPEC] * 3,
         [
             pltpu.VMEM((parts, RANK, tokens // parts), F32),
             pltpu.VMEM((half, inputs.shape[1]), BF16),
@@ -136,13 +139,16 @@
     )
 
 
-def error_product_kernel(q_hbm, e_hbm, p_ref, q_ref, q3_ref, e_ref, sem, sems):
+def error_product_kernel(core_ref, q_hbm, e_hbm, p_ref, q_ref, q3_ref, e_ref, sem, sems):
     step = 768
     q_copy = pltpu.make_async_copy(q_hbm, q_ref, sem)
     q_copy.start()
     start_rows(e_hbm, e_ref, sems, step)
-    q_copy.wait()
-    q3_ref[...] = three_terms(q_ref[...])
+
+    @pl.when(core_ref[0] >= 0)
+    def _():
+        q_copy.wait()
+        q3_ref[...] = three_terms(q_ref[...])
 
     def work(i):
         rows = pl.ds(pl.multiple_of(i * step, step), step)
@@ -151,10 +157,10 @@
     for_rows(e_hbm, e_ref, sems, step, work)
 
 
-def error_product(q_t, error):
+def error_product(core, q_t, error):
     rows, cols = error.shape
     return call(
-        error_product_kernel, "error_product", (there(q_t), there(error)), [HBM_SPEC] * 2,
+        error_product_kernel, "error_product", (core, there(q_t), there(error)), [SMEM_SPEC] + [HBM_SPEC] * 2,
         pltpu.VMEM((RANK, rows), F32), VMEM_SPEC, 16,
         [
             pltpu.VMEM(q_t.shape, F32),
@@ -255,19 +261,16 @@
     )(at, *arrays)
 
 
-def load_kernel(g_hbm, e_hbm, g_ref, e_ref, sems):
-    copies = [pltpu.make_async_copy(g_hbm, g_ref, sems.at[0]), pltpu.make_async_copy(e_hbm, e_ref, sems.at[1])]
-    for copy in copies:
-        copy.start()
-    for copy in copies:
-        copy.wait()
-
-
-def loaded(grads, error):
-    return call(
-        load_kernel, "loaded", (there(grads), there(error)), [HBM_SPEC] * 2,
-        [pltpu.VMEM(grads.shape, BF16), pltpu.VMEM(error.shape, BF16)], [VMEM_SPEC] * 2, 12,
-        [pltpu.SemaphoreType.DMA((2,))], 0, 2 * (grads.size + error.size),
+def load_kernel(source, target, sem):
+    copy = pltpu.make_async_copy(source, target, sem)
+    copy.start()
+    copy.wait()
+
+
+def loaded(x, cost):
+    return call(
+        load_kernel, "loaded", (there(x),), [HBM_SPEC], pltpu.VMEM(x.shape, x.dtype), VMEM_SPEC, 12,
+        [pltpu.SemaphoreType.DMA], cost, 0,
     )
 
 
@@ -302,7 +305,8 @@
         factor = jnp.where(row > k, both[:, k:k + 1] / pivot, 0.0)
         both = both - factor * both[k:k + 1, :]
     inverse = both[:, RANK:] * scale
-    inv_ref[...] = inverse
+    i1, i2, i3 = (term.astype(F32) for term in split3(inverse))
+    inv_ref[...] = jnp.concatenate([i1, i1, i1, i2, i2, i3], axis=1).astype(BF16)
     u = lax.dot_general(inverse, p, NN, precision=lax.Precision.HIGHEST, preferred_element_type=F32)
     u1, u2, u3 = (term.astype(F32) for term in split3(u))
     u6 = jnp.concatenate([u1, u2, u3, u1, u2, u1, u, jnp.zeros_like(u)], axis=0).T
@@ -314,7 +318,7 @@
     rows = p.shape[1]
     return call(
         factor_kernel, "factor", (here(p),), [VMEM_SPEC],
-        [pltpu.VMEM((RANK, rows), F32), pltpu.VMEM((rows, 6 * RANK), BF16), pltpu.VMEM((RANK, RANK), F32)],
+        [pltpu.VMEM((RANK, rows), F32), pltpu.VMEM((rows, 6 * RANK), BF16), pltpu.VMEM((RANK, 6 * RANK), BF16)],
         [VMEM_SPEC] * 3, 12, (), 4e9, 0,
     )
 
@@ -322,8 +326,8 @@
 def residual_kernel(replicas, core_ref, mine_ref, other_ref, inv_ref, u_ref, *refs):
     *c_refs, out_hbm, q_ref, full_ref, w6_ref, block_ref, sems = refs
     join_halves(core_ref[0], mine_ref, other_ref, full_ref)
-    w = lax.dot_general(inv_ref[...], full_ref[...], NN, precision=lax.Precision.HIGHEST, preferred_element_type=F32)
-    w = w * (1.0 / replicas)
+    q1, q2, q3 = split3(full_ref[...])
+    w = dot(inv_ref[...], jnp.concatenate([q1, q2, q3, q1, q2, q1], axis=0), NN) * (1.0 / replicas)
     q_ref[...] = w
     w1, w2, w3 = split3(-w)
     w6_ref[...] = jnp.concatenate([w1, w1, w1, w2, w2, w3], axis=0)
@@ -407,39 +411,39 @@
     core = lax.axis_index("c").astype(jnp.int32)[None]
     at = lax.axis_index("z").astype(jnp.int32)[None]
     replicas = 32
-    tokens, top, bottom = token_product(q_start.T, grads, inputs, 4)
+    tokens, top, bottom = token_product(core, q_start.T, grads, inputs, 4)
     (q_t,) = after(tokens, q_start.T)
     tokens = lax.all_to_all(tokens, "z", 0, 0)
     left_a, right_b = shift(top, 1), shift(bottom, -1)
-    error_part = error_product(q_t, error)
+    error_part = error_product(core, q_t, error)
     keep, send = left_partial(core, tokens, inputs, error_part)
     p = keep + swap(send, "c", [(0, 1)])
+    p = add_swapped(p, "z", FIRST)
     bottom, top = after(p, bottom, top)
     left_b, right_a = shift(bottom, 1), shift(top, -1)
-    p = add_swapped(p, "x", FIRST)
-    inputs_t = turned(((0, 0), (3, 0), (1, 1)), at, after(p, inputs, left_a, right_b))
-    p = add_swapped(p, "x", SECOND, inputs_t)
+    inputs_t = turned(((0, 0), (3, 0), (1, 1)), at, after(p, inputs, left_a, right_b), None, 4e9)
+    p = add_swapped(p, "z", SECOND, inputs_t)
     far_a, far_b = after(p, left_a, right_b)
     far_a, far_b = shift(far_a, 1), shift(far_b, -1)
-    p = add_swapped(p, "y", FIRST)
-    grads, error = loaded(*after(p, grads, error))
-    p = add_swapped(p, "y", SECOND, grads, error)
-    left_b, right_a, inputs_t = after(p, left_b, right_a, inputs_t)
-    inputs_t = turned(((3, 1), (1, 0)), at, (left_b, right_a), inputs_t, 4e9)
-    p = add_swapped(p, "z", FIRST, inputs_t)
+    p = add_swapped(p, "x", FIRST)
+    error = loaded(*after(p, error), 4e9)
+    p = add_swapped(p, "x", SECOND, error)
+    left_b, right_a, inputs_t, grads = after(p, left_b, right_a, inputs_t, grads)
+    grads = loaded(grads, 2e9)
+    inputs_t = turned(((3, 1), (1, 0)), at, (left_b, right_a), inputs_t, 2e9)
+    p = add_swapped(p, "y", FIRST, grads, inputs_t)
     far_a, far_b, inputs_t = after(p, far_a, far_b, inputs_t)
-    inputs_t = turned(((2, 0), (2, 1)), at, (far_a, far_b), inputs_t)
-    part = lambda s, reason: combined(s, 4, *after(reason, inputs_t, grads, error))
-    parts = [part(0, p)]
-    p = add_swapped(p, "z", SECOND, parts[0])
+    inputs_t = turned(((2, 0), (2, 1)), at, (far_a, far_b), inputs_t, 0)
+    p = add_swapped(p, "y", SECOND, inputs_t)
     keep, send, p = right_partial(core, p, swap(p, "c", [(0, 1)]), inputs_t, grads, error)
 
     q = keep + swap(send, "c", [(0, 1)])
-    for s, (axis, pairs) in enumerate((("x", FIRST), ("x", SECOND), ("y", FIRST))):
-        parts.append(part(s + 1, q))
+    basis, u6, inverse = factor(*after(q, p))
+    q = add_swapped(q, "x", FIRST, basis)
+    parts = []
+    for s, (axis, pairs) in enumerate((("x", SECOND), ("y", FIRST), ("y", SECOND))):
+        parts.append(combined(s, 3, *after(q, inputs_t, grads, error)))
         q = add_swapped(q, axis, pairs, parts[-1])
-    basis, u6, inverse = factor(*after(q, p))
-    q = add_swapped(q, "y", SECOND, basis)
     other = swap(q, "c", [(0, 1)])
     error_next, q_next = residual(core, q, other, inverse, u6, parts, replicas)
     return error_next, basis.T, q_next.T

time: 104 us -> 103 us (level)
  waiting for transfers between devices: 16.2 us -> 17.8 us
  starting transfers between devices: 39.6 us -> 38.2 us
    ppermute x6, waiting for transfers between devices: 0.02 us -> 6.61 us  [shift(): return lax.ppermute(x, 'z', [(i, (i + by) % 4) for i in range(4)])]
    ppermute x14, waiting for transfers between devices: 16.2 us -> 11.2 us  [swap(): lax.ppermute(x, axis, [(a, b) for a, b in pairs] + [(b, a) for a, b in pa...]
    ppermute x14, starting transfers between devices: 25.7 us -> 24.3 us  [swap(): lax.ppermute(x, axis, [(a, b) for a, b in pairs] + [(b, a) for a, b in pa...]
    pallas_call x3, Pallas kernels: 2.79 us -> 1.55 us  [turned(): pl.pallas_call(functools.partial(turn_kernel, places), in_specs=[SMEM_SPE...]
where the time goes in v3:
time: 103 us
  Pallas kernels  44.9 us (44%)
  starting transfers between devices  38.2 us (37%)
  waiting for transfers between devices  17.8 us (17%)
    pallas_call x11, Pallas kernels, call(): pl.pallas_call(kernel, in_specs=in_specs, out_specs=out_specs, out_shape=...  43.4 us
    ppermute x14, starting transfers between devices, swap(): lax.ppermute(x, axis, [(a, b) for a, b in pairs] + [(b, a) for a, b in pa...  24.3 us
    ppermute x14, waiting for transfers between devices, swap(): lax.ppermute(x, axis, [(a, b) for a, b in pairs] + [(b, a) for a, b in pa...  11.2 us
    ppermute x6, starting transfers between devices, shift(): return lax.ppermute(x, 'z', [(i, (i + by) % 4) for i in range(4)])  8.06 us
    ppermute x6, waiting for transfers between devices, shift(): return lax.ppermute(x, 'z', [(i, (i + by) % 4) for i in range(4)])  6.61 us
    all_to_all x1, starting transfers between devices, local(): tokens = lax.all_to_all(tokens, 'z', 0, 0)  5.87 us
  transfers between devices with their start and end apart: 21, of which 10 were waited for; matrix products, arithmetic and copies ran while one was open for 1% of the time, Pallas kernels for 30%

profile of v3, /device:TPU:1, one launch (start us, length us, event | category | flops | bytes accessed | tf_op | source)
XLA Modules:
  0.0 102.9 jit_solution(9403472347141342044)
XLA Ops:
  0.6 4.4 %token_product.1 = (f32[4,32,256]{2,1,0:T(8,128)}, bf16[128,2304]{1,0:T(8,128)(2,1)S(1)}, bf16[128,2304]{1,0:T(8,128)(2,1)}) custom-call(s32[1]{0:T(128)} %bitcast.core_ref, f32[32,2304]{1,0:T(8,128)} %bitcast.16, bf16[1024,2304]{1,0:T(8,128)(2,1)} %bitcast.12, bf16[256,2304]{1,0:T(8,128)(2,1)} %bitcast.9), custom_call_target="tpu_custom_call" | custom-call | flops 1207959552 | bytes 4718592 | tf_op jit(solution)/shard_map/token_product/pallas_call | solution.py:51
  5.0 5.9 %all-to-all-start = ((f32[4,32,256]{2,1,0:T(8,128)}), f32[4,32,256]{2,1,0:T(8,128)S(1)}, u32[]{:S(2)}, u32[]{:S(2)}) async-start(f32[4,32,256]{2,1,0:T(8,128)} %get-tuple-element.50), calls=%async_computation | async-start | bytes 262144 | tf_op jit(solution)/shard_map/all_to_all | solution.py:416
  10.9 1.5 %collective-permute-start.3 = (bf16[128,2304]{1,0:T(8,128)(2,1)S(1)}, bf16[128,2304]{1,0:T(8,128)(2,1)S(1)}, u32[]{:S(2)}, u32[]{:S(2)}) collective-permute-start(bf16[128,2304]{1,0:T(8,128)(2,1)S(1)} %get-tuple-element.63), channel_id=1, source_target_pairs={{0,1},{1,2},{2,3},{3,0},{4,5},{5,6},{6,7},{7,4},{8,9},{9,10},{10,1... | collective-permute-start | bytes 1769480 | tf_op jit(solution)/shard_map/ppermute | solution.py:394
  13.6 6.8 %error_product.1.e_ref = f32[32,2304]{1,0:T(8,128)S(1)} custom-call(s32[1]{0:T(128)} %bitcast.core_ref, f32[32,2304]{1,0:T(8,128)} %bitcast.17, bf16[2304,2304]{1,0:T(8,128)(2,1)} %bitcast.14), custom_call_target="tpu_custom_call" | custom-call | flops 10000000000 | tf_op jit(solution)/shard_map/error_product/pallas_call | solution.py:51
  20.9 1.6 %collective-permute-start = (f32[36,8,128]{2,1,0:T(8,128)S(1)}, f32[36,8,128]{2,1,0:T(8,128)S(1)}, u32[]{:S(2)}, u32[]{:S(2)}) collective-permute-start(f32[36,8,128]{2,1,0:T(8,128)S(1)} %get-tuple-element.53), channel_id=1, source_target_pairs={{0,4},{4,0},{1,5},{5,1},{2,6},{6,2},{3,7},{7,3},{8,12},{12,8},{9,1... | collective-permute-start | bytes 442376 | tf_op jit(solution)/shard_map/ppermute | solution.py:390
  24.1 6.3 %collective-permute-done.1 = f32[36,8,128]{2,1,0:T(8,128)S(1)} collective-permute-done((f32[36,8,128]{2,1,0:T(8,128)S(1)}, f32[36,8,128]{2,1,0:T(8,128)S(1)}, u32[]{:S(2)}, u32[]{:S(2)}) %collective-permute-start.1) | collective-permute-done | bytes 147488 | tf_op jit(solution)/shard_map/ppermute | solution.py:390
  32.5 1.6 %collective-permute-start.9 = (bf16[128,2304]{1,0:T(8,128)(2,1)S(1)}, bf16[128,2304]{1,0:T(8,128)(2,1)S(1)}, u32[]{:S(2)}, u32[]{:S(2)}) collective-permute-start(bf16[128,2304]{1,0:T(8,128)(2,1)S(1)} %get-tuple-element.63), channel_id=1, source_target_pairs={{0,3},{1,0},{2,1},{3,2},{4,7},{5,4},{6,5},{7,6},{8,11},{9,8},{10,9... | collective-permute-start | bytes 1769480 | tf_op jit(solution)/shard_map/ppermute | solution.py:394
  37.0 2.7 %collective-permute-start.12 = (bf16[128,2304]{1,0:T(8,128)(2,1)S(1)}, bf16[128,2304]{1,0:T(8,128)(2,1)S(1)}, u32[]{:S(2)}, u32[]{:S(2)}) collective-permute-start(bf16[128,2304]{1,0:T(8,128)(2,1)S(1)} %collective-permute-done.4.refs_2_), channel_id=1, source_target_pairs={{0,3},{1,0},{2,1},{3,2},{4,7},{5,4},{6,5},{7,6},{8,11},{9,8},{10,9... | collective-permute-start | bytes 1769480 | tf_op jit(solution)/shard_map/ppermute | solution.py:394
  40.1 2.6 %collective-permute-start.6 = (f32[36,8,128]{2,1,0:T(8,128)S(1)}, f32[36,8,128]{2,1,0:T(8,128)S(1)}, u32[]{:S(2)}, u32[]{:S(2)}) collective-permute-start(f32[36,8,128]{2,1,0:T(8,128)S(1)} %add.39), channel_id=1, source_target_pairs={{32,64},{96,0},{64,32},{0,96},{33,65},{97,1},{65,33},{1,97},{34,66... | collective-permute-start | bytes 442376 | tf_op jit(solution)/shard_map/ppermute | solution.py:390
  42.6 4.0 %loaded.2.e_ref = bf16[2304,2304]{1,0:T(8,128)(2,1)S(1)} custom-call(bf16[2304,2304]{1,0:T(8,128)(2,1)} %bitcast.15), custom_call_target="tpu_custom_call" | custom-call | flops 4000000000 | tf_op jit(solution)/shard_map/loaded/pallas_call | solution.py:51
  46.7 1.4 %collective-permute-start.7 = (f32[36,8,128]{2,1,0:T(8,128)S(1)}, f32[36,8,128]{2,1,0:T(8,128)S(1)}, u32[]{:S(2)}, u32[]{:S(2)}) collective-permute-start(f32[36,8,128]{2,1,0:T(8,128)S(1)} %add.40), channel_id=1, source_target_pairs={{0,8},{16,24},{8,0},{24,16},{1,9},{17,25},{9,1},{25,17},{2,10},{18... | collective-permute-start | bytes 442376 | tf_op jit(solution)/shard_map/ppermute | solution.py:390
  48.1 2.3 %loaded.3.g_ref = bf16[1024,2304]{1,0:T(8,128)(2,1)S(1)} custom-call(bf16[1024,2304]{1,0:T(8,128)(2,1)} %bitcast.13), custom_call_target="tpu_custom_call" | custom-call | flops 2000000000 | tf_op jit(solution)/shard_map/loaded/pallas_call | solution.py:51
  51.1 2.8 %collective-permute-start.10 = (f32[36,8,128]{2,1,0:T(8,128)S(1)}, f32[36,8,128]{2,1,0:T(8,128)S(1)}, u32[]{:S(2)}, u32[]{:S(2)}) collective-permute-start(f32[36,8,128]{2,1,0:T(8,128)S(1)} %add.41), channel_id=1, source_target_pairs={{8,16},{24,0},{16,8},{0,24},{9,17},{25,1},{17,9},{1,25},{10,18},{2... | collective-permute-start | bytes 442376 | tf_op jit(solution)/shard_map/ppermute | solution.py:390
  53.9 6.6 %collective-permute-done.11.refs_0_ = bf16[128,2304]{1,0:T(8,128)(2,1)S(1)} collective-permute-done((bf16[128,2304]{1,0:T(8,128)(2,1)S(1)}, bf16[128,2304]{1,0:T(8,128)(2,1)S(1)}, u32[]{:S(2)}, u32[]{:S(2)}) %collective-permute-start.11) | collective-permute-done | bytes 589856 | tf_op jit(solution)/shard_map/ppermute | solution.py:394
  60.9 3.2 %collective-permute-start.13 = (f32[36,8,128]{2,1,0:T(8,128)S(1)}, f32[36,8,128]{2,1,0:T(8,128)S(1)}, u32[]{:S(2)}, u32[]{:S(2)}) collective-permute-start(f32[36,8,128]{2,1,0:T(8,128)S(1)} %add.42.mine_ref), channel_id=1, source_target_pairs={{0,4},{4,0},{1,5},{5,1},{2,6},{6,2},{3,7},{7,3},{8,12},{12,8},{9,1... | collective-permute-start | bytes 442376 | tf_op jit(solution)/shard_map/ppermute | solution.py:390
  65.2 3.7 %right_partial.1 = (f32[36,8,128]{2,1,0:T(8,128)S(1)}, f32[36,8,128]{2,1,0:T(8,128)S(1)}, f32[32,2304]{1,0:T(8,128)S(1)}) custom-call(s32[1]{0:T(128)} %bitcast.core_ref, f32[36,8,128]{2,1,0:T(8,128)S(1)} %add.42.mine_ref, f32[36,8,128]{2,1,0:T(8,128)S(1)} %collective-permute-done.13.other_ref, bf16[2304,1024]{1,0:T(8,128)(2,1)S(1)} %turned.5.xt_ref, ...), custom_call_target="tpu_custom_call" | custom-call | flops 5133828096 | tf_op jit(solution)/shard_map/right_partial/pallas_call | solution.py:51
  71.3 4.1 %factor.1 = (f32[32,2304]{1,0:T(8,128)S(1)}, bf16[2304,192]{1,0:T(8,128)(2,1)S(1)}, bf16[32,192]{1,0:T(8,128)(2,1)S(1)}) custom-call(f32[32,2304]{1,0:T(8,128)S(1)} %get-tuple-element.78.p_ref), custom_call_target="tpu_custom_call" | custom-call | flops 4000000000 | tf_op jit(solution)/shard_map/factor/pallas_call | solution.py:51
  75.7 2.1 %collective-permute-start.16 = (f32[36,8,128]{2,1,0:T(8,128)S(1)}, f32[36,8,128]{2,1,0:T(8,128)S(1)}, u32[]{:S(2)}, u32[]{:S(2)}) collective-permute-start(f32[36,8,128]{2,1,0:T(8,128)S(1)} %add.44), channel_id=1, source_target_pairs={{32,64},{96,0},{64,32},{0,96},{33,65},{97,1},{65,33},{1,97},{34,66... | collective-permute-start | bytes 442376 | tf_op jit(solution)/shard_map/ppermute | solution.py:390
  77.8 3.8 %combined.3.refs_0_ = f32[768,2304]{1,0:T(8,128)S(1)} custom-call(bf16[2304,1024]{1,0:T(8,128)(2,1)S(1)} %turned.5.xt_ref, bf16[1024,2304]{1,0:T(8,128)(2,1)S(1)} %loaded.3.g_ref, bf16[2304,2304]{1,0:T(8,128)(2,1)S(1)} %loaded.2.e_ref), custom_call_target="tpu_custom_call" | custom-call | flops 3623878656 | tf_op jit(solution)/shard_map/combined/pallas_call | solution.py:51
  83.0 3.8 %combined.4.refs_1_ = f32[768,2304]{1,0:T(8,128)S(1)} custom-call(bf16[2304,1024]{1,0:T(8,128)(2,1)S(1)} %turned.5.xt_ref, bf16[1024,2304]{1,0:T(8,128)(2,1)S(1)} %loaded.3.g_ref, bf16[2304,2304]{1,0:T(8,128)(2,1)S(1)} %loaded.2.e_ref), custom_call_target="tpu_custom_call" | custom-call | flops 3623878656 | tf_op jit(solution)/shard_map/combined/pallas_call | solution.py:51
  86.9 2.0 %collective-permute-start.18 = (f32[36,8,128]{2,1,0:T(8,128)S(1)}, f32[36,8,128]{2,1,0:T(8,128)S(1)}, u32[]{:S(2)}, u32[]{:S(2)}) collective-permute-start(f32[36,8,128]{2,1,0:T(8,128)S(1)} %add.46), channel_id=1, source_target_pairs={{8,16},{24,0},{16,8},{0,24},{9,17},{25,1},{17,9},{1,25},{10,18},{2... | collective-permute-start | bytes 442376 | tf_op jit(solution)/shard_map/ppermute | solution.py:390
  88.9 3.8 %combined.5.refs_2_ = f32[768,2304]{1,0:T(8,128)S(1)} custom-call(bf16[2304,1024]{1,0:T(8,128)(2,1)S(1)} %turned.5.xt_ref, bf16[1024,2304]{1,0:T(8,128)(2,1)S(1)} %loaded.3.g_ref, bf16[2304,2304]{1,0:T(8,128)(2,1)S(1)} %loaded.2.e_ref), custom_call_target="tpu_custom_call" | custom-call | flops 3623878656 | tf_op jit(solution)/shard_map/combined/pallas_call | solution.py:51
  92.8 2.8 %collective-permute-start.19 = (f32[36,8,128]{2,1,0:T(8,128)S(1)}, f32[36,8,128]{2,1,0:T(8,128)S(1)}, u32[]{:S(2)}, u32[]{:S(2)}) collective-permute-start(f32[36,8,128]{2,1,0:T(8,128)S(1)} %add.47.mine_ref), channel_id=1, source_target_pairs={{0,4},{4,0},{1,5},{5,1},{2,6},{6,2},{3,7},{7,3},{8,12},{12,8},{9,1... | collective-permute-start | bytes 442376 | tf_op jit(solution)/shard_map/ppermute | solution.py:390
  96.6 6.1 %residual.1 = (bf16[1,2304,2304]{2,1,0:T(8,128)(2,1)}, f32[32,2304]{1,0:T(8,128)}) custom-call(s32[1]{0:T(128)} %bitcast.core_ref, f32[36,8,128]{2,1,0:T(8,128)S(1)} %add.47.mine_ref, f32[36,8,128]{2,1,0:T(8,128)S(1)} %collective-permute-done.19.other_ref, bf16[32,192]{1,0:T(8,128)(2,1)S(1)} %get-tuple-element.93.inv_ref, ...), custom_call_target="tpu_custom_call" | custom-call | flops 2717908992 | bytes 10616832 | tf_op jit(solution)/shard_map/residual/pallas_call | solution.py:51
  (47 shorter events, 15.9 us)
Async XLA Ops:
  5.0 15.4 %all-to-all-start = ((f32[4,32,256]{2,1,0:T(8,128)}), f32[4,32,256]{2,1,0:T(8,128)S(1)}, u32[]{:S(2)}, u32[]{:S(2)}) async-start(f32[4,32,256]{2,1,0:T(8,128)} %get-tuple-element.50), calls=%async_computation | async-start | bytes 262144 | tf_op jit(solution)/shard_map/all_to_all | solution.py:416
  10.9 23.2 %collective-permute-start.3 = (bf16[128,2304]{1,0:T(8,128)(2,1)S(1)}, bf16[128,2304]{1,0:T(8,128)(2,1)S(1)}, u32[]{:S(2)}, u32[]{:S(2)}) collective-permute-start(bf16[128,2304]{1,0:T(8,128)(2,1)S(1)} %get-tuple-element.63), channel_id=1, source_target_pairs={{0,1},{1,2},{2,3},{3,0},{4,5},{5,6},{6,7},{7,4},{8,9},{9,10},{10,1... | collective-permute-start | bytes 1769480 | tf_op jit(solution)/shard_map/ppermute | solution.py:394
  12.4 21.8 %collective-permute-start.4 = (bf16[128,2304]{1,0:T(8,128)(2,1)}, bf16[128,2304]{1,0:T(8,128)(2,1)S(1)}, u32[]{:S(2)}, u32[]{:S(2)}) collective-permute-start(bf16[128,2304]{1,0:T(8,128)(2,1)} %get-tuple-element.62), channel_id=1, source_target_pairs={{0,3},{1,0},{2,1},{3,2},{4,7},{5,4},{6,5},{7,6},{8,11},{9,8},{10,9... | collective-permute-start | bytes 1769480 | tf_op jit(solution)/shard_map/ppermute | solution.py:394
  13.6 6.9 %copy-start = (bf16[1,256,2304]{2,1,0:T(8,128)(2,1)S(1)}, bf16[1,256,2304]{2,1,0:T(8,128)(2,1)}, u32[]{:S(2)}) copy-start(bf16[1,256,2304]{2,1,0:T(8,128)(2,1)} %param.4) | copy-start | bytes 3538948
  20.9 2.6 %collective-permute-start = (f32[36,8,128]{2,1,0:T(8,128)S(1)}, f32[36,8,128]{2,1,0:T(8,128)S(1)}, u32[]{:S(2)}, u32[]{:S(2)}) collective-permute-start(f32[36,8,128]{2,1,0:T(8,128)S(1)} %get-tuple-element.53), channel_id=1, source_target_pairs={{0,4},{4,0},{1,5},{5,1},{2,6},{6,2},{3,7},{7,3},{8,12},{12,8},{9,1... | collective-permute-start | bytes 442376 | tf_op jit(solution)/shard_map/ppermute | solution.py:390
  23.5 6.9 %collective-permute-start.1 = (f32[36,8,128]{2,1,0:T(8,128)S(1)}, f32[36,8,128]{2,1,0:T(8,128)S(1)}, u32[]{:S(2)}, u32[]{:S(2)}) collective-permute-start(f32[36,8,128]{2,1,0:T(8,128)S(1)} %add.36), channel_id=1, source_target_pairs={{0,1},{2,3},{1,0},{3,2},{4,5},{6,7},{5,4},{7,6},{8,9},{10,11},{9,8... | collective-permute-start | bytes 442376 | tf_op jit(solution)/shard_map/ppermute | solution.py:390
  30.4 5.3 %collective-permute-start.2 = (f32[36,8,128]{2,1,0:T(8,128)S(1)}, f32[36,8,128]{2,1,0:T(8,128)S(1)}, u32[]{:S(2)}, u32[]{:S(2)}) collective-permute-start(f32[36,8,128]{2,1,0:T(8,128)S(1)} %add.37), channel_id=1, source_target_pairs={{1,2},{3,0},{2,1},{0,3},{5,6},{7,4},{6,5},{4,7},{9,10},{11,8},{10,... | collective-permute-start | bytes 442376 | tf_op jit(solution)/shard_map/ppermute | solution.py:390
  31.4 16.6 %collective-permute-start.8 = (bf16[128,2304]{1,0:T(8,128)(2,1)}, bf16[128,2304]{1,0:T(8,128)(2,1)S(1)}, u32[]{:S(2)}, u32[]{:S(2)}) collective-permute-start(bf16[128,2304]{1,0:T(8,128)(2,1)} %get-tuple-element.62), channel_id=1, source_target_pairs={{0,1},{1,2},{2,3},{3,0},{4,5},{5,6},{6,7},{7,4},{8,9},{9,10},{10,1... | collective-permute-start | bytes 1769480 | tf_op jit(solution)/shard_map/ppermute | solution.py:394
  32.5 15.6 %collective-permute-start.9 = (bf16[128,2304]{1,0:T(8,128)(2,1)S(1)}, bf16[128,2304]{1,0:T(8,128)(2,1)S(1)}, u32[]{:S(2)}, u32[]{:S(2)}) collective-permute-start(bf16[128,2304]{1,0:T(8,128)(2,1)S(1)} %get-tuple-element.63), channel_id=1, source_target_pairs={{0,3},{1,0},{2,1},{3,2},{4,7},{5,4},{6,5},{7,6},{8,11},{9,8},{10,9... | collective-permute-start | bytes 1769480 | tf_op jit(solution)/shard_map/ppermute | solution.py:394
  35.7 4.4 %collective-permute-start.5 = (f32[36,8,128]{2,1,0:T(8,128)S(1)}, f32[36,8,128]{2,1,0:T(8,128)S(1)}, u32[]{:S(2)}, u32[]{:S(2)}) collective-permute-start(f32[36,8,128]{2,1,0:T(8,128)S(1)} %add.38), channel_id=1, source_target_pairs={{0,32},{64,96},{32,0},{96,64},{1,33},{65,97},{33,1},{97,65},{2,34}... | collective-permute-start | bytes 442376 | tf_op jit(solution)/shard_map/ppermute | solution.py:390
  37.0 23.5 %collective-permute-start.11 = (bf16[128,2304]{1,0:T(8,128)(2,1)S(1)}, bf16[128,2304]{1,0:T(8,128)(2,1)S(1)}, u32[]{:S(2)}, u32[]{:S(2)}) collective-permute-start(bf16[128,2304]{1,0:T(8,128)(2,1)S(1)} %collective-permute-done.3.refs_1_), channel_id=1, source_target_pairs={{0,1},{1,2},{2,3},{3,0},{4,5},{5,6},{6,7},{7,4},{8,9},{9,10},{10,1... | collective-permute-start | bytes 1769480 | tf_op jit(solution)/shard_map/ppermute | solution.py:394
  37.0 23.5 %collective-permute-start.12 = (bf16[128,2304]{1,0:T(8,128)(2,1)S(1)}, bf16[128,2304]{1,0:T(8,128)(2,1)S(1)}, u32[]{:S(2)}, u32[]{:S(2)}) collective-permute-start(bf16[128,2304]{1,0:T(8,128)(2,1)S(1)} %collective-permute-done.4.refs_2_), channel_id=1, source_target_pairs={{0,3},{1,0},{2,1},{3,2},{4,7},{5,4},{6,5},{7,6},{8,11},{9,8},{10,9... | collective-permute-start | bytes 1769480 | tf_op jit(solution)/shard_map/ppermute | solution.py:394
  40.1 6.6 %collective-permute-start.6 = (f32[36,8,128]{2,1,0:T(8,128)S(1)}, f32[36,8,128]{2,1,0:T(8,128)S(1)}, u32[]{:S(2)}, u32[]{:S(2)}) collective-permute-start(f32[36,8,128]{2,1,0:T(8,128)S(1)} %add.39), channel_id=1, source_target_pairs={{32,64},{96,0},{64,32},{0,96},{33,65},{97,1},{65,33},{1,97},{34,66... | collective-permute-start | bytes 442376 | tf_op jit(solution)/shard_map/ppermute | solution.py:390
  46.7 4.4 %collective-permute-start.7 = (f32[36,8,128]{2,1,0:T(8,128)S(1)}, f32[36,8,128]{2,1,0:T(8,128)S(1)}, u32[]{:S(2)}, u32[]{:S(2)}) collective-permute-start(f32[36,8,128]{2,1,0:T(8,128)S(1)} %add.40), channel_id=1, source_target_pairs={{0,8},{16,24},{8,0},{24,16},{1,9},{17,25},{9,1},{25,17},{2,10},{18... | collective-permute-start | bytes 442376 | tf_op jit(solution)/shard_map/ppermute | solution.py:390
  51.1 9.8 %collective-permute-start.10 = (f32[36,8,128]{2,1,0:T(8,128)S(1)}, f32[36,8,128]{2,1,0:T(8,128)S(1)}, u32[]{:S(2)}, u32[]{:S(2)}) collective-permute-start(f32[36,8,128]{2,1,0:T(8,128)S(1)} %add.41), channel_id=1, source_target_pairs={{8,16},{24,0},{16,8},{0,24},{9,17},{25,1},{17,9},{1,25},{10,18},{2... | collective-permute-start | bytes 442376 | tf_op jit(solution)/shard_map/ppermute | solution.py:390
  60.9 4.3 %collective-permute-start.13 = (f32[36,8,128]{2,1,0:T(8,128)S(1)}, f32[36,8,128]{2,1,0:T(8,128)S(1)}, u32[]{:S(2)}, u32[]{:S(2)}) collective-permute-start(f32[36,8,128]{2,1,0:T(8,128)S(1)} %add.42.mine_ref), channel_id=1, source_target_pairs={{0,4},{4,0},{1,5},{5,1},{2,6},{6,2},{3,7},{7,3},{8,12},{12,8},{9,1... | collective-permute-start | bytes 442376 | tf_op jit(solution)/shard_map/ppermute | solution.py:390
  68.9 1.5 %collective-permute-start.14 = (f32[36,8,128]{2,1,0:T(8,128)S(1)}, f32[36,8,128]{2,1,0:T(8,128)S(1)}, u32[]{:S(2)}, u32[]{:S(2)}) collective-permute-start(f32[36,8,128]{2,1,0:T(8,128)S(1)} %get-tuple-element.76), channel_id=1, source_target_pairs={{0,4},{4,0},{1,5},{5,1},{2,6},{6,2},{3,7},{7,3},{8,12},{12,8},{9,1... | collective-permute-start | bytes 442376 | tf_op jit(solution)/shard_map/ppermute | solution.py:390
  70.3 5.3 %collective-permute-start.15 = (f32[36,8,128]{2,1,0:T(8,128)S(1)}, f32[36,8,128]{2,1,0:T(8,128)S(1)}, u32[]{:S(2)}, u32[]{:S(2)}) collective-permute-start(f32[36,8,128]{2,1,0:T(8,128)S(1)} %add.43), channel_id=1, source_target_pairs={{0,32},{64,96},{32,0},{96,64},{1,33},{65,97},{33,1},{97,65},{2,34}... | collective-permute-start | bytes 442376 | tf_op jit(solution)/shard_map/ppermute | solution.py:390
  75.7 6.0 %collective-permute-start.16 = (f32[36,8,128]{2,1,0:T(8,128)S(1)}, f32[36,8,128]{2,1,0:T(8,128)S(1)}, u32[]{:S(2)}, u32[]{:S(2)}) collective-permute-start(f32[36,8,128]{2,1,0:T(8,128)S(1)} %add.44), channel_id=1, source_target_pairs={{32,64},{96,0},{64,32},{0,96},{33,65},{97,1},{65,33},{1,97},{34,66... | collective-permute-start | bytes 442376 | tf_op jit(solution)/shard_map/ppermute | solution.py:390
  81.7 5.2 %collective-permute-start.17 = (f32[36,8,128]{2,1,0:T(8,128)S(1)}, f32[36,8,128]{2,1,0:T(8,128)S(1)}, u32[]{:S(2)}, u32[]{:S(2)}) collective-permute-start(f32[36,8,128]{2,1,0:T(8,128)S(1)} %add.45), channel_id=1, source_target_pairs={{0,8},{16,24},{8,0},{24,16},{1,9},{17,25},{9,1},{25,17},{2,10},{18... | collective-permute-start | bytes 442376 | tf_op jit(solution)/shard_map/ppermute | solution.py:390
  86.9 5.8 %collective-permute-start.18 = (f32[36,8,128]{2,1,0:T(8,128)S(1)}, f32[36,8,128]{2,1,0:T(8,128)S(1)}, u32[]{:S(2)}, u32[]{:S(2)}) collective-permute-start(f32[36,8,128]{2,1,0:T(8,128)S(1)} %add.46), channel_id=1, source_target_pairs={{8,16},{24,0},{16,8},{0,24},{9,17},{25,1},{17,9},{1,25},{10,18},{2... | collective-permute-start | bytes 442376 | tf_op jit(solution)/shard_map/ppermute | solution.py:390
  92.8 3.8 %collective-permute-start.19 = (f32[36,8,128]{2,1,0:T(8,128)S(1)}, f32[36,8,128]{2,1,0:T(8,128)S(1)}, u32[]{:S(2)}, u32[]{:S(2)}) collective-permute-start(f32[36,8,128]{2,1,0:T(8,128)S(1)} %add.47.mine_ref), channel_id=1, source_target_pairs={{0,4},{4,0},{1,5},{5,1},{2,6},{6,2},{3,7},{7,3},{8,12},{12,8},{9,1... | collective-permute-start | bytes 442376 | tf_op jit(solution)/shard_map/ppermute | solution.py:390

commit v4 on v3

--- a/solution.py
+++ b/solution.py
@@ -99,8 +99,6 @@
     ]
     q_copy.start()
     start_rows(g_hbm, g_ref, g_sems, step)
-    for copy in halves:
-        copy.start()
 
     @pl.when(core_ref[0] >= 0)
     def _():
@@ -108,6 +106,11 @@
         q3_ref[...] = three_terms(q_ref[...])
 
     def work(i):
+        @pl.when(i == 0)
+        def _():
+            for copy in halves:
+                copy.start()
+
         for k in range(step // part):
             rows = pl.ds(pl.multiple_of(i * step + k * part, part), part)
             t_ref[i * (step // part) + k] = turned_fold(dot(g_ref[rows, :], q3_ref[...], NN))

time: 103 us -> 103 us (level)
  no operation moved by 1% of the time
where the time goes in v4:
time: 103 us
  Pallas kernels  45 us (44%)
  starting transfers between devices  38.2 us (37%)
  waiting for transfers between devices  17.8 us (17%)
    pallas_call x11, Pallas kernels, call(): pl.pallas_call(kernel, in_specs=in_specs, out_specs=out_specs, out_shape=...  43.4 us
    ppermute x14, starting transfers between devices, swap(): lax.ppermute(x, axis, [(a, b) for a, b in pairs] + [(b, a) for a, b in pa...  24.3 us
    ppermute x14, waiting for transfers between devices, swap(): lax.ppermute(x, axis, [(a, b) for a, b in pairs] + [(b, a) for a, b in pa...  11.2 us
    ppermute x6, starting transfers between devices, shift(): return lax.ppermute(x, 'z', [(i, (i + by) % 4) for i in range(4)])  8.06 us
    ppermute x6, waiting for transfers between devices, shift(): return lax.ppermute(x, 'z', [(i, (i + by) % 4) for i in range(4)])  6.61 us
    all_to_all x1, starting transfers between devices, local(): tokens = lax.all_to_all(tokens, 'z', 0, 0)  5.87 us
  transfers between devices with their start and end apart: 21, of which 10 were waited for; matrix products, arithmetic and copies ran while one was open for 1% of the time, Pallas kernels for 30%

profile of v4, /device:TPU:1, one launch (start us, length us, event | category | flops | bytes accessed | tf_op | source)
XLA Modules:
  0.0 103.0 jit_solution(7491001980461025098)
XLA Ops:
  0.6 4.5 %token_product.1 = (f32[4,32,256]{2,1,0:T(8,128)}, bf16[128,2304]{1,0:T(8,128)(2,1)S(1)}, bf16[128,2304]{1,0:T(8,128)(2,1)}) custom-call(s32[1]{0:T(128)} %bitcast.core_ref, f32[32,2304]{1,0:T(8,128)} %bitcast.16, bf16[1024,2304]{1,0:T(8,128)(2,1)} %bitcast.12, bf16[256,2304]{1,0:T(8,128)(2,1)} %bitcast.9), custom_call_target="tpu_custom_call" | custom-call | flops 1207959552 | bytes 4718592 | tf_op jit(solution)/shard_map/token_product/pallas_call | solution.py:51
  5.1 5.9 %all-to-all-start = ((f32[4,32,256]{2,1,0:T(8,128)}), f32[4,32,256]{2,1,0:T(8,128)S(1)}, u32[]{:S(2)}, u32[]{:S(2)}) async-start(f32[4,32,256]{2,1,0:T(8,128)} %get-tuple-element.50), calls=%async_computation | async-start | bytes 262144 | tf_op jit(solution)/shard_map/all_to_all | solution.py:419
  11.0 1.5 %collective-permute-start.3 = (bf16[128,2304]{1,0:T(8,128)(2,1)S(1)}, bf16[128,2304]{1,0:T(8,128)(2,1)S(1)}, u32[]{:S(2)}, u32[]{:S(2)}) collective-permute-start(bf16[128,2304]{1,0:T(8,128)(2,1)S(1)} %get-tuple-element.63), channel_id=1, source_target_pairs={{0,1},{1,2},{2,3},{3,0},{4,5},{5,6},{6,7},{7,4},{8,9},{9,10},{10,1... | collective-permute-start | bytes 1769480 | tf_op jit(solution)/shard_map/ppermute | solution.py:397
  13.7 6.8 %error_product.1.e_ref = f32[32,2304]{1,0:T(8,128)S(1)} custom-call(s32[1]{0:T(128)} %bitcast.core_ref, f32[32,2304]{1,0:T(8,128)} %bitcast.17, bf16[2304,2304]{1,0:T(8,128)(2,1)} %bitcast.14), custom_call_target="tpu_custom_call" | custom-call | flops 10000000000 | tf_op jit(solution)/shard_map/error_product/pallas_call | solution.py:51
  20.9 1.6 %collective-permute-start = (f32[36,8,128]{2,1,0:T(8,128)S(1)}, f32[36,8,128]{2,1,0:T(8,128)S(1)}, u32[]{:S(2)}, u32[]{:S(2)}) collective-permute-start(f32[36,8,128]{2,1,0:T(8,128)S(1)} %get-tuple-element.53), channel_id=1, source_target_pairs={{0,4},{4,0},{1,5},{5,1},{2,6},{6,2},{3,7},{7,3},{8,12},{12,8},{9,1... | collective-permute-start | bytes 442376 | tf_op jit(solution)/shard_map/ppermute | solution.py:393
  24.1 6.3 %collective-permute-done.1 = f32[36,8,128]{2,1,0:T(8,128)S(1)} collective-permute-done((f32[36,8,128]{2,1,0:T(8,128)S(1)}, f32[36,8,128]{2,1,0:T(8,128)S(1)}, u32[]{:S(2)}, u32[]{:S(2)}) %collective-permute-start.1) | collective-permute-done | bytes 147488 | tf_op jit(solution)/shard_map/ppermute | solution.py:393
  32.6 1.6 %collective-permute-start.9 = (bf16[128,2304]{1,0:T(8,128)(2,1)S(1)}, bf16[128,2304]{1,0:T(8,128)(2,1)S(1)}, u32[]{:S(2)}, u32[]{:S(2)}) collective-permute-start(bf16[128,2304]{1,0:T(8,128)(2,1)S(1)} %get-tuple-element.63), channel_id=1, source_target_pairs={{0,3},{1,0},{2,1},{3,2},{4,7},{5,4},{6,5},{7,6},{8,11},{9,8},{10,9... | collective-permute-start | bytes 1769480 | tf_op jit(solution)/shard_map/ppermute | solution.py:397
  37.1 2.7 %collective-permute-start.12 = (bf16[128,2304]{1,0:T(8,128)(2,1)S(1)}, bf16[128,2304]{1,0:T(8,128)(2,1)S(1)}, u32[]{:S(2)}, u32[]{:S(2)}) collective-permute-start(bf16[128,2304]{1,0:T(8,128)(2,1)S(1)} %collective-permute-done.4.refs_2_), channel_id=1, source_target_pairs={{0,3},{1,0},{2,1},{3,2},{4,7},{5,4},{6,5},{7,6},{8,11},{9,8},{10,9... | collective-permute-start | bytes 1769480 | tf_op jit(solution)/shard_map/ppermute | solution.py:397
  40.2 2.6 %collective-permute-start.6 = (f32[36,8,128]{2,1,0:T(8,128)S(1)}, f32[36,8,128]{2,1,0:T(8,128)S(1)}, u32[]{:S(2)}, u32[]{:S(2)}) collective-permute-start(f32[36,8,128]{2,1,0:T(8,128)S(1)} %add.39), channel_id=1, source_target_pairs={{32,64},{96,0},{64,32},{0,96},{33,65},{97,1},{65,33},{1,97},{34,66... | collective-permute-start | bytes 442376 | tf_op jit(solution)/shard_map/ppermute | solution.py:393
  42.7 4.0 %loaded.2.e_ref = bf16[2304,2304]{1,0:T(8,128)(2,1)S(1)} custom-call(bf16[2304,2304]{1,0:T(8,128)(2,1)} %bitcast.15), custom_call_target="tpu_custom_call" | custom-call | flops 4000000000 | tf_op jit(solution)/shard_map/loaded/pallas_call | solution.py:51
  48.2 2.3 %loaded.3.g_ref = bf16[1024,2304]{1,0:T(8,128)(2,1)S(1)} custom-call(bf16[1024,2304]{1,0:T(8,128)(2,1)} %bitcast.13), custom_call_target="tpu_custom_call" | custom-call | flops 2000000000 | tf_op jit(solution)/shard_map/loaded/pallas_call | solution.py:51
  51.2 2.8 %collective-permute-start.10 = (f32[36,8,128]{2,1,0:T(8,128)S(1)}, f32[36,8,128]{2,1,0:T(8,128)S(1)}, u32[]{:S(2)}, u32[]{:S(2)}) collective-permute-start(f32[36,8,128]{2,1,0:T(8,128)S(1)} %add.41), channel_id=1, source_target_pairs={{8,16},{24,0},{16,8},{0,24},{9,17},{25,1},{17,9},{1,25},{10,18},{2... | collective-permute-start | bytes 442376 | tf_op jit(solution)/shard_map/ppermute | solution.py:393
  54.0 6.6 %collective-permute-done.11.refs_0_ = bf16[128,2304]{1,0:T(8,128)(2,1)S(1)} collective-permute-done((bf16[128,2304]{1,0:T(8,128)(2,1)S(1)}, bf16[128,2304]{1,0:T(8,128)(2,1)S(1)}, u32[]{:S(2)}, u32[]{:S(2)}) %collective-permute-start.11) | collective-permute-done | bytes 589856 | tf_op jit(solution)/shard_map/ppermute | solution.py:397
  61.0 3.2 %collective-permute-start.13 = (f32[36,8,128]{2,1,0:T(8,128)S(1)}, f32[36,8,128]{2,1,0:T(8,128)S(1)}, u32[]{:S(2)}, u32[]{:S(2)}) collective-permute-start(f32[36,8,128]{2,1,0:T(8,128)S(1)} %add.42.mine_ref), channel_id=1, source_target_pairs={{0,4},{4,0},{1,5},{5,1},{2,6},{6,2},{3,7},{7,3},{8,12},{12,8},{9,1... | collective-permute-start | bytes 442376 | tf_op jit(solution)/shard_map/ppermute | solution.py:393
  65.3 3.7 %right_partial.1 = (f32[36,8,128]{2,1,0:T(8,128)S(1)}, f32[36,8,128]{2,1,0:T(8,128)S(1)}, f32[32,2304]{1,0:T(8,128)S(1)}) custom-call(s32[1]{0:T(128)} %bitcast.core_ref, f32[36,8,128]{2,1,0:T(8,128)S(1)} %add.42.mine_ref, f32[36,8,128]{2,1,0:T(8,128)S(1)} %collective-permute-done.13.other_ref, bf16[2304,1024]{1,0:T(8,128)(2,1)S(1)} %turned.5.xt_ref, ...), custom_call_target="tpu_custom_call" | custom-call | flops 5133828096 | tf_op jit(solution)/shard_map/right_partial/pallas_call | solution.py:51
  71.4 4.1 %factor.1 = (f32[32,2304]{1,0:T(8,128)S(1)}, bf16[2304,192]{1,0:T(8,128)(2,1)S(1)}, bf16[32,192]{1,0:T(8,128)(2,1)S(1)}) custom-call(f32[32,2304]{1,0:T(8,128)S(1)} %get-tuple-element.78.p_ref), custom_call_target="tpu_custom_call" | custom-call | flops 4000000000 | tf_op jit(solution)/shard_map/factor/pallas_call | solution.py:51
  75.8 2.1 %collective-permute-start.16 = (f32[36,8,128]{2,1,0:T(8,128)S(1)}, f32[36,8,128]{2,1,0:T(8,128)S(1)}, u32[]{:S(2)}, u32[]{:S(2)}) collective-permute-start(f32[36,8,128]{2,1,0:T(8,128)S(1)} %add.44), channel_id=1, source_target_pairs={{32,64},{96,0},{64,32},{0,96},{33,65},{97,1},{65,33},{1,97},{34,66... | collective-permute-start | bytes 442376 | tf_op jit(solution)/shard_map/ppermute | solution.py:393
  77.9 3.8 %combined.3.refs_0_ = f32[768,2304]{1,0:T(8,128)S(1)} custom-call(bf16[2304,1024]{1,0:T(8,128)(2,1)S(1)} %turned.5.xt_ref, bf16[1024,2304]{1,0:T(8,128)(2,1)S(1)} %loaded.3.g_ref, bf16[2304,2304]{1,0:T(8,128)(2,1)S(1)} %loaded.2.e_ref), custom_call_target="tpu_custom_call" | custom-call | flops 3623878656 | tf_op jit(solution)/shard_map/combined/pallas_call | solution.py:51
  81.7 1.4 %collective-permute-start.17 = (f32[36,8,128]{2,1,0:T(8,128)S(1)}, f32[36,8,128]{2,1,0:T(8,128)S(1)}, u32[]{:S(2)}, u32[]{:S(2)}) collective-permute-start(f32[36,8,128]{2,1,0:T(8,128)S(1)} %add.45), channel_id=1, source_target_pairs={{0,8},{16,24},{8,0},{24,16},{1,9},{17,25},{9,1},{25,17},{2,10},{18... | collective-permute-start | bytes 442376 | tf_op jit(solution)/shard_map/ppermute | solution.py:393
  83.1 3.8 %combined.4.refs_1_ = f32[768,2304]{1,0:T(8,128)S(1)} custom-call(bf16[2304,1024]{1,0:T(8,128)(2,1)S(1)} %turned.5.xt_ref, bf16[1024,2304]{1,0:T(8,128)(2,1)S(1)} %loaded.3.g_ref, bf16[2304,2304]{1,0:T(8,128)(2,1)S(1)} %loaded.2.e_ref), custom_call_target="tpu_custom_call" | custom-call | flops 3623878656 | tf_op jit(solution)/shard_map/combined/pallas_call | solution.py:51
  87.0 2.0 %collective-permute-start.18 = (f32[36,8,128]{2,1,0:T(8,128)S(1)}, f32[36,8,128]{2,1,0:T(8,128)S(1)}, u32[]{:S(2)}, u32[]{:S(2)}) collective-permute-start(f32[36,8,128]{2,1,0:T(8,128)S(1)} %add.46), channel_id=1, source_target_pairs={{8,16},{24,0},{16,8},{0,24},{9,17},{25,1},{17,9},{1,25},{10,18},{2... | collective-permute-start | bytes 442376 | tf_op jit(solution)/shard_map/ppermute | solution.py:393
  89.0 3.8 %combined.5.refs_2_ = f32[768,2304]{1,0:T(8,128)S(1)} custom-call(bf16[2304,1024]{1,0:T(8,128)(2,1)S(1)} %turned.5.xt_ref, bf16[1024,2304]{1,0:T(8,128)(2,1)S(1)} %loaded.3.g_ref, bf16[2304,2304]{1,0:T(8,128)(2,1)S(1)} %loaded.2.e_ref), custom_call_target="tpu_custom_call" | custom-call | flops 3623878656 | tf_op jit(solution)/shard_map/combined/pallas_call | solution.py:51
  92.9 2.9 %collective-permute-start.19 = (f32[36,8,128]{2,1,0:T(8,128)S(1)}, f32[36,8,128]{2,1,0:T(8,128)S(1)}, u32[]{:S(2)}, u32[]{:S(2)}) collective-permute-start(f32[36,8,128]{2,1,0:T(8,128)S(1)} %add.47.mine_ref), channel_id=1, source_target_pairs={{0,4},{4,0},{1,5},{5,1},{2,6},{6,2},{3,7},{7,3},{8,12},{12,8},{9,1... | collective-permute-start | bytes 442376 | tf_op jit(solution)/shard_map/ppermute | solution.py:393
  96.7 6.1 %residual.1 = (bf16[1,2304,2304]{2,1,0:T(8,128)(2,1)}, f32[32,2304]{1,0:T(8,128)}) custom-call(s32[1]{0:T(128)} %bitcast.core_ref, f32[36,8,128]{2,1,0:T(8,128)S(1)} %add.47.mine_ref, f32[36,8,128]{2,1,0:T(8,128)S(1)} %collective-permute-done.19.other_ref, bf16[32,192]{1,0:T(8,128)(2,1)S(1)} %get-tuple-element.93.inv_ref, ...), custom_call_target="tpu_custom_call" | custom-call | flops 2717908992 | bytes 10616832 | tf_op jit(solution)/shard_map/residual/pallas_call | solution.py:51
  (47 shorter events, 15.9 us)
Async XLA Ops:
  5.1 15.4 %all-to-all-start = ((f32[4,32,256]{2,1,0:T(8,128)}), f32[4,32,256]{2,1,0:T(8,128)S(1)}, u32[]{:S(2)}, u32[]{:S(2)}) async-start(f32[4,32,256]{2,1,0:T(8,128)} %get-tuple-element.50), calls=%async_computation | async-start | bytes 262144 | tf_op jit(solution)/shard_map/all_to_all | solution.py:419
  11.0 23.2 %collective-permute-start.3 = (bf16[128,2304]{1,0:T(8,128)(2,1)S(1)}, bf16[128,2304]{1,0:T(8,128)(2,1)S(1)}, u32[]{:S(2)}, u32[]{:S(2)}) collective-permute-start(bf16[128,2304]{1,0:T(8,128)(2,1)S(1)} %get-tuple-element.63), channel_id=1, source_target_pairs={{0,1},{1,2},{2,3},{3,0},{4,5},{5,6},{6,7},{7,4},{8,9},{9,10},{10,1... | collective-permute-start | bytes 1769480 | tf_op jit(solution)/shard_map/ppermute | solution.py:397
  12.5 21.8 %collective-permute-start.4 = (bf16[128,2304]{1,0:T(8,128)(2,1)}, bf16[128,2304]{1,0:T(8,128)(2,1)S(1)}, u32[]{:S(2)}, u32[]{:S(2)}) collective-permute-start(bf16[128,2304]{1,0:T(8,128)(2,1)} %get-tuple-element.62), channel_id=1, source_target_pairs={{0,3},{1,0},{2,1},{3,2},{4,7},{5,4},{6,5},{7,6},{8,11},{9,8},{10,9... | collective-permute-start | bytes 1769480 | tf_op jit(solution)/shard_map/ppermute | solution.py:397
  13.7 6.9 %copy-start = (bf16[1,256,2304]{2,1,0:T(8,128)(2,1)S(1)}, bf16[1,256,2304]{2,1,0:T(8,128)(2,1)}, u32[]{:S(2)}) copy-start(bf16[1,256,2304]{2,1,0:T(8,128)(2,1)} %param.4) | copy-start | bytes 3538948
  20.9 2.6 %collective-permute-start = (f32[36,8,128]{2,1,0:T(8,128)S(1)}, f32[36,8,128]{2,1,0:T(8,128)S(1)}, u32[]{:S(2)}, u32[]{:S(2)}) collective-permute-start(f32[36,8,128]{2,1,0:T(8,128)S(1)} %get-tuple-element.53), channel_id=1, source_target_pairs={{0,4},{4,0},{1,5},{5,1},{2,6},{6,2},{3,7},{7,3},{8,12},{12,8},{9,1... | collective-permute-start | bytes 442376 | tf_op jit(solution)/shard_map/ppermute | solution.py:393
  23.6 6.9 %collective-permute-start.1 = (f32[36,8,128]{2,1,0:T(8,128)S(1)}, f32[36,8,128]{2,1,0:T(8,128)S(1)}, u32[]{:S(2)}, u32[]{:S(2)}) collective-permute-start(f32[36,8,128]{2,1,0:T(8,128)S(1)} %add.36), channel_id=1, source_target_pairs={{0,1},{2,3},{1,0},{3,2},{4,5},{6,7},{5,4},{7,6},{8,9},{10,11},{9,8... | collective-permute-start | bytes 442376 | tf_op jit(solution)/shard_map/ppermute | solution.py:393
  30.5 5.3 %collective-permute-start.2 = (f32[36,8,128]{2,1,0:T(8,128)S(1)}, f32[36,8,128]{2,1,0:T(8,128)S(1)}, u32[]{:S(2)}, u32[]{:S(2)}) collective-permute-start(f32[36,8,128]{2,1,0:T(8,128)S(1)} %add.37), channel_id=1, source_target_pairs={{1,2},{3,0},{2,1},{0,3},{5,6},{7,4},{6,5},{4,7},{9,10},{11,8},{10,... | collective-permute-start | bytes 442376 | tf_op jit(solution)/shard_map/ppermute | solution.py:393
  31.5 16.6 %collective-permute-start.8 = (bf16[128,2304]{1,0:T(8,128)(2,1)}, bf16[128,2304]{1,0:T(8,128)(2,1)S(1)}, u32[]{:S(2)}, u32[]{:S(2)}) collective-permute-start(bf16[128,2304]{1,0:T(8,128)(2,1)} %get-tuple-element.62), channel_id=1, source_target_pairs={{0,1},{1,2},{2,3},{3,0},{4,5},{5,6},{6,7},{7,4},{8,9},{9,10},{10,1... | collective-permute-start | bytes 1769480 | tf_op jit(solution)/shard_map/ppermute | solution.py:397
  32.6 15.6 %collective-permute-start.9 = (bf16[128,2304]{1,0:T(8,128)(2,1)S(1)}, bf16[128,2304]{1,0:T(8,128)(2,1)S(1)}, u32[]{:S(2)}, u32[]{:S(2)}) collective-permute-start(bf16[128,2304]{1,0:T(8,128)(2,1)S(1)} %get-tuple-element.63), channel_id=1, source_target_pairs={{0,3},{1,0},{2,1},{3,2},{4,7},{5,4},{6,5},{7,6},{8,11},{9,8},{10,9... | collective-permute-start | bytes 1769480 | tf_op jit(solution)/shard_map/ppermute | solution.py:397
  35.8 4.4 %collective-permute-start.5 = (f32[36,8,128]{2,1,0:T(8,128)S(1)}, f32[36,8,128]{2,1,0:T(8,128)S(1)}, u32[]{:S(2)}, u32[]{:S(2)}) collective-permute-start(f32[36,8,128]{2,1,0:T(8,128)S(1)} %add.38), channel_id=1, source_target_pairs={{0,32},{64,96},{32,0},{96,64},{1,33},{65,97},{33,1},{97,65},{2,34}... | collective-permute-start | bytes 442376 | tf_op jit(solution)/shard_map/ppermute | solution.py:393
  37.0 23.5 %collective-permute-start.11 = (bf16[128,2304]{1,0:T(8,128)(2,1)S(1)}, bf16[128,2304]{1,0:T(8,128)(2,1)S(1)}, u32[]{:S(2)}, u32[]{:S(2)}) collective-permute-start(bf16[128,2304]{1,0:T(8,128)(2,1)S(1)} %collective-permute-done.3.refs_1_), channel_id=1, source_target_pairs={{0,1},{1,2},{2,3},{3,0},{4,5},{5,6},{6,7},{7,4},{8,9},{9,10},{10,1... | collective-permute-start | bytes 1769480 | tf_op jit(solution)/shard_map/ppermute | solution.py:397
  37.1 23.5 %collective-permute-start.12 = (bf16[128,2304]{1,0:T(8,128)(2,1)S(1)}, bf16[128,2304]{1,0:T(8,128)(2,1)S(1)}, u32[]{:S(2)}, u32[]{:S(2)}) collective-permute-start(bf16[128,2304]{1,0:T(8,128)(2,1)S(1)} %collective-permute-done.4.refs_2_), channel_id=1, source_target_pairs={{0,3},{1,0},{2,1},{3,2},{4,7},{5,4},{6,5},{7,6},{8,11},{9,8},{10,9... | collective-permute-start | bytes 1769480 | tf_op jit(solution)/shard_map/ppermute | solution.py:397
  40.2 6.6 %collective-permute-start.6 = (f32[36,8,128]{2,1,0:T(8,128)S(1)}, f32[36,8,128]{2,1,0:T(8,128)S(1)}, u32[]{:S(2)}, u32[]{:S(2)}) collective-permute-start(f32[36,8,128]{2,1,0:T(8,128)S(1)} %add.39), channel_id=1, source_target_pairs={{32,64},{96,0},{64,32},{0,96},{33,65},{97,1},{65,33},{1,97},{34,66... | collective-permute-start | bytes 442376 | tf_op jit(solution)/shard_map/ppermute | solution.py:393
  46.8 4.4 %collective-permute-start.7 = (f32[36,8,128]{2,1,0:T(8,128)S(1)}, f32[36,8,128]{2,1,0:T(8,128)S(1)}, u32[]{:S(2)}, u32[]{:S(2)}) collective-permute-start(f32[36,8,128]{2,1,0:T(8,128)S(1)} %add.40), channel_id=1, source_target_pairs={{0,8},{16,24},{8,0},{24,16},{1,9},{17,25},{9,1},{25,17},{2,10},{18... | collective-permute-start | bytes 442376 | tf_op jit(solution)/shard_map/ppermute | solution.py:393
  51.2 9.8 %collective-permute-start.10 = (f32[36,8,128]{2,1,0:T(8,128)S(1)}, f32[36,8,128]{2,1,0:T(8,128)S(1)}, u32[]{:S(2)}, u32[]{:S(2)}) collective-permute-start(f32[36,8,128]{2,1,0:T(8,128)S(1)} %add.41), channel_id=1, source_target_pairs={{8,16},{24,0},{16,8},{0,24},{9,17},{25,1},{17,9},{1,25},{10,18},{2... | collective-permute-start | bytes 442376 | tf_op jit(solution)/shard_map/ppermute | solution.py:393
  61.0 4.3 %collective-permute-start.13 = (f32[36,8,128]{2,1,0:T(8,128)S(1)}, f32[36,8,128]{2,1,0:T(8,128)S(1)}, u32[]{:S(2)}, u32[]{:S(2)}) collective-permute-start(f32[36,8,128]{2,1,0:T(8,128)S(1)} %add.42.mine_ref), channel_id=1, source_target_pairs={{0,4},{4,0},{1,5},{5,1},{2,6},{6,2},{3,7},{7,3},{8,12},{12,8},{9,1... | collective-permute-start | bytes 442376 | tf_op jit(solution)/shard_map/ppermute | solution.py:393
  68.9 1.5 %collective-permute-start.14 = (f32[36,8,128]{2,1,0:T(8,128)S(1)}, f32[36,8,128]{2,1,0:T(8,128)S(1)}, u32[]{:S(2)}, u32[]{:S(2)}) collective-permute-start(f32[36,8,128]{2,1,0:T(8,128)S(1)} %get-tuple-element.76), channel_id=1, source_target_pairs={{0,4},{4,0},{1,5},{5,1},{2,6},{6,2},{3,7},{7,3},{8,12},{12,8},{9,1... | collective-permute-start | bytes 442376 | tf_op jit(solution)/shard_map/ppermute | solution.py:393
  70.4 5.3 %collective-permute-start.15 = (f32[36,8,128]{2,1,0:T(8,128)S(1)}, f32[36,8,128]{2,1,0:T(8,128)S(1)}, u32[]{:S(2)}, u32[]{:S(2)}) collective-permute-start(f32[36,8,128]{2,1,0:T(8,128)S(1)} %add.43), channel_id=1, source_target_pairs={{0,32},{64,96},{32,0},{96,64},{1,33},{65,97},{33,1},{97,65},{2,34}... | collective-permute-start | bytes 442376 | tf_op jit(solution)/shard_map/ppermute | solution.py:393
  75.8 5.9 %collective-permute-start.16 = (f32[36,8,128]{2,1,0:T(8,128)S(1)}, f32[36,8,128]{2,1,0:T(8,128)S(1)}, u32[]{:S(2)}, u32[]{:S(2)}) collective-permute-start(f32[36,8,128]{2,1,0:T(8,128)S(1)} %add.44), channel_id=1, source_target_pairs={{32,64},{96,0},{64,32},{0,96},{33,65},{97,1},{65,33},{1,97},{34,66... | collective-permute-start | bytes 442376 | tf_op jit(solution)/shard_map/ppermute | solution.py:393
  81.7 5.2 %collective-permute-start.17 = (f32[36,8,128]{2,1,0:T(8,128)S(1)}, f32[36,8,128]{2,1,0:T(8,128)S(1)}, u32[]{:S(2)}, u32[]{:S(2)}) collective-permute-start(f32[36,8,128]{2,1,0:T(8,128)S(1)} %add.45), channel_id=1, source_target_pairs={{0,8},{16,24},{8,0},{24,16},{1,9},{17,25},{9,1},{25,17},{2,10},{18... | collective-permute-start | bytes 442376 | tf_op jit(solution)/shard_map/ppermute | solution.py:393
  87.0 5.8 %collective-permute-start.18 = (f32[36,8,128]{2,1,0:T(8,128)S(1)}, f32[36,8,128]{2,1,0:T(8,128)S(1)}, u32[]{:S(2)}, u32[]{:S(2)}) collective-permute-start(f32[36,8,128]{2,1,0:T(8,128)S(1)} %add.46), channel_id=1, source_target_pairs={{8,16},{24,0},{16,8},{0,24},{9,17},{25,1},{17,9},{1,25},{10,18},{2... | collective-permute-start | bytes 442376 | tf_op jit(solution)/shard_map/ppermute | solution.py:393
  92.9 3.9 %collective-permute-start.19 = (f32[36,8,128]{2,1,0:T(8,128)S(1)}, f32[36,8,128]{2,1,0:T(8,128)S(1)}, u32[]{:S(2)}, u32[]{:S(2)}) collective-permute-start(f32[36,8,128]{2,1,0:T(8,128)S(1)} %add.47.mine_ref), channel_id=1, source_target_pairs={{0,4},{4,0},{1,5},{5,1},{2,6},{6,2},{3,7},{7,3},{8,12},{12,8},{9,1... | collective-permute-start | bytes 442376 | tf_op jit(solution)/shard_map/ppermute | solution.py:393

commit v5 on v3

--- a/solution.py
+++ b/solution.py
@@ -418,7 +418,8 @@
     error_part = error_product(core, q_t, error)
     keep, send = left_partial(core, tokens, inputs, error_part)
     p = keep + swap(send, "c", [(0, 1)])
-    p = add_swapped(p, "z", FIRST)
+    error = loaded(*after(p, error), 4e9)
+    p = add_swapped(p, "z", FIRST, error)
     bottom, top = after(p, bottom, top)
     left_b, right_a = shift(bottom, 1), shift(top, -1)
     inputs_t = turned(((0, 0), (3, 0), (1, 1)), at, after(p, inputs, left_a, right_b), None, 4e9)
@@ -426,8 +427,7 @@
     far_a, far_b = after(p, left_a, right_b)
     far_a, far_b = shift(far_a, 1), shift(far_b, -1)
     p = add_swapped(p, "x", FIRST)
-    error = loaded(*after(p, error), 4e9)
-    p = add_swapped(p, "x", SECOND, error)
+    p = add_swapped(p, "x", SECOND)
     left_b, right_a, inputs_t, grads = after(p, left_b, right_a, inputs_t, grads)
     grads = loaded(grads, 2e9)
     inputs_t = turned(((3, 1), (1, 0)), at, (left_b, right_a), inputs_t, 2e9)

time: 103 us -> 103 us (level)
    ppermute x14, waiting for transfers between devices: 11.2 us -> 8.57 us  [swap(): lax.ppermute(x, axis, [(a, b) for a, b in pairs] + [(b, a) for a, b in pa...]
    ppermute x6, waiting for transfers between devices: 6.61 us -> 8.22 us  [shift(): return lax.ppermute(x, 'z', [(i, (i + by) % 4) for i in range(4)])]
where the time goes in v5:
time: 103 us
  Pallas kernels  45.6 us (44%)
  starting transfers between devices  38.7 us (38%)
  waiting for transfers between devices  16.8 us (16%)
  between operations  1.03 us (1%)
    pallas_call x11, Pallas kernels, call(): pl.pallas_call(kernel, in_specs=in_specs, out_specs=out_specs, out_shape=...  44 us
    ppermute x14, starting transfers between devices, swap(): lax.ppermute(x, axis, [(a, b) for a, b in pairs] + [(b, a) for a, b in pa...  24.8 us
    ppermute x14, waiting for transfers between devices, swap(): lax.ppermute(x, axis, [(a, b) for a, b in pairs] + [(b, a) for a, b in pa...  8.57 us
    ppermute x6, waiting for transfers between devices, shift(): return lax.ppermute(x, 'z', [(i, (i + by) % 4) for i in range(4)])  8.22 us
    ppermute x6, starting transfers between devices, shift(): return lax.ppermute(x, 'z', [(i, (i + by) % 4) for i in range(4)])  8.06 us
    all_to_all x1, starting transfers between devices, local(): tokens = lax.all_to_all(tokens, 'z', 0, 0)  5.87 us
  transfers between devices with their start and end apart: 21, of which 10 were waited for; matrix products, arithmetic and copies ran while one was open for 1% of the time, Pallas kernels for 30%

profile of v5, /device:TPU:1, one launch (start us, length us, event | category | flops | bytes accessed | tf_op | source)
XLA Modules:
  0.0 103.0 jit_solution(8448054801387974585)
XLA Ops:
  0.6 4.4 %token_product.1 = (f32[4,32,256]{2,1,0:T(8,128)}, bf16[128,2304]{1,0:T(8,128)(2,1)S(1)}, bf16[128,2304]{1,0:T(8,128)(2,1)}) custom-call(s32[1]{0:T(128)} %bitcast.core_ref, f32[32,2304]{1,0:T(8,128)} %bitcast.16, bf16[1024,2304]{1,0:T(8,128)(2,1)} %bitcast.12, bf16[256,2304]{1,0:T(8,128)(2,1)} %bitcast.9), custom_call_target="tpu_custom_call" | custom-call | flops 1207959552 | bytes 4718592 | tf_op jit(solution)/shard_map/token_product/pallas_call | solution.py:51
  5.0 5.9 %all-to-all-start = ((f32[4,32,256]{2,1,0:T(8,128)}), f32[4,32,256]{2,1,0:T(8,128)S(1)}, u32[]{:S(2)}, u32[]{:S(2)}) async-start(f32[4,32,256]{2,1,0:T(8,128)} %get-tuple-element.50), calls=%async_computation | async-start | bytes 262144 | tf_op jit(solution)/shard_map/all_to_all | solution.py:416
  13.6 6.8 %error_product.1.e_ref = f32[32,2304]{1,0:T(8,128)S(1)} custom-call(s32[1]{0:T(128)} %bitcast.core_ref, f32[32,2304]{1,0:T(8,128)} %bitcast.17, bf16[2304,2304]{1,0:T(8,128)(2,1)} %bitcast.14), custom_call_target="tpu_custom_call" | custom-call | flops 10000000000 | tf_op jit(solution)/shard_map/error_product/pallas_call | solution.py:51
  21.5 1.5 %collective-permute-start = (f32[36,8,128]{2,1,0:T(8,128)}, f32[36,8,128]{2,1,0:T(8,128)S(1)}, u32[]{:S(2)}, u32[]{:S(2)}) collective-permute-start(f32[36,8,128]{2,1,0:T(8,128)} %get-tuple-element.53), channel_id=1, source_target_pairs={{0,4},{4,0},{1,5},{5,1},{2,6},{6,2},{3,7},{7,3},{8,12},{12,8},{9,1... | collective-permute-start | bytes 442376 | tf_op jit(solution)/shard_map/ppermute | solution.py:390
  24.8 4.0 %loaded.2.e_ref = bf16[2304,2304]{1,0:T(8,128)(2,1)S(1)} custom-call(bf16[2304,2304]{1,0:T(8,128)(2,1)} %bitcast.15), custom_call_target="tpu_custom_call" | custom-call | flops 4000000000 | tf_op jit(solution)/shard_map/loaded/pallas_call | solution.py:51
  28.9 1.5 %collective-permute-done.1 = f32[36,8,128]{2,1,0:T(8,128)S(1)} collective-permute-done((f32[36,8,128]{2,1,0:T(8,128)S(1)}, f32[36,8,128]{2,1,0:T(8,128)S(1)}, u32[]{:S(2)}, u32[]{:S(2)}) %collective-permute-start.1) | collective-permute-done | bytes 147488 | tf_op jit(solution)/shard_map/ppermute | solution.py:390
  30.4 1.7 %collective-permute-start.2 = (f32[36,8,128]{2,1,0:T(8,128)S(1)}, f32[36,8,128]{2,1,0:T(8,128)S(1)}, u32[]{:S(2)}, u32[]{:S(2)}) collective-permute-start(f32[36,8,128]{2,1,0:T(8,128)S(1)} %add.37), channel_id=1, source_target_pairs={{1,2},{3,0},{2,1},{0,3},{5,6},{7,4},{6,5},{4,7},{9,10},{11,8},{10,... | collective-permute-start | bytes 442376 | tf_op jit(solution)/shard_map/ppermute | solution.py:390
  32.5 2.2 %collective-permute-start.9 = (bf16[128,2304]{1,0:T(8,128)(2,1)S(1)}, bf16[128,2304]{1,0:T(8,128)(2,1)S(1)}, u32[]{:S(2)}, u32[]{:S(2)}) collective-permute-start(bf16[128,2304]{1,0:T(8,128)(2,1)S(1)} %get-tuple-element.63), channel_id=1, source_target_pairs={{0,3},{1,0},{2,1},{3,2},{4,7},{5,4},{6,5},{7,6},{8,11},{9,8},{10,9... | collective-permute-start | bytes 1769480 | tf_op jit(solution)/shard_map/ppermute | solution.py:394
  37.0 3.1 %collective-permute-done.5 = f32[36,8,128]{2,1,0:T(8,128)S(1)} collective-permute-done((f32[36,8,128]{2,1,0:T(8,128)S(1)}, f32[36,8,128]{2,1,0:T(8,128)S(1)}, u32[]{:S(2)}, u32[]{:S(2)}) %collective-permute-start.5) | collective-permute-done | bytes 147488 | tf_op jit(solution)/shard_map/ppermute | solution.py:390
  40.1 2.6 %collective-permute-start.6 = (f32[36,8,128]{2,1,0:T(8,128)S(1)}, f32[36,8,128]{2,1,0:T(8,128)S(1)}, u32[]{:S(2)}, u32[]{:S(2)}) collective-permute-start(f32[36,8,128]{2,1,0:T(8,128)S(1)} %add.39), channel_id=1, source_target_pairs={{32,64},{96,0},{64,32},{0,96},{33,65},{97,1},{65,33},{1,97},{34,66... | collective-permute-start | bytes 442376 | tf_op jit(solution)/shard_map/ppermute | solution.py:390
  42.6 2.7 %collective-permute-start.12 = (bf16[128,2304]{1,0:T(8,128)(2,1)S(1)}, bf16[128,2304]{1,0:T(8,128)(2,1)S(1)}, u32[]{:S(2)}, u32[]{:S(2)}) collective-permute-start(bf16[128,2304]{1,0:T(8,128)(2,1)S(1)} %collective-permute-done.4.refs_2_), channel_id=1, source_target_pairs={{0,3},{1,0},{2,1},{3,2},{4,7},{5,4},{6,5},{7,6},{8,11},{9,8},{10,9... | collective-permute-start | bytes 1769480 | tf_op jit(solution)/shard_map/ppermute | solution.py:394
  48.5 2.3 %loaded.3.g_ref = bf16[1024,2304]{1,0:T(8,128)(2,1)S(1)} custom-call(bf16[1024,2304]{1,0:T(8,128)(2,1)} %bitcast.13), custom_call_target="tpu_custom_call" | custom-call | flops 2000000000 | tf_op jit(solution)/shard_map/loaded/pallas_call | solution.py:51
  51.3 2.8 %collective-permute-start.10 = (f32[36,8,128]{2,1,0:T(8,128)S(1)}, f32[36,8,128]{2,1,0:T(8,128)S(1)}, u32[]{:S(2)}, u32[]{:S(2)}) collective-permute-start(f32[36,8,128]{2,1,0:T(8,128)S(1)} %add.41), channel_id=1, source_target_pairs={{8,16},{24,0},{16,8},{0,24},{9,17},{25,1},{17,9},{1,25},{10,18},{2... | collective-permute-start | bytes 442376 | tf_op jit(solution)/shard_map/ppermute | solution.py:390
  54.1 6.7 %collective-permute-done.11.refs_0_ = bf16[128,2304]{1,0:T(8,128)(2,1)S(1)} collective-permute-done((bf16[128,2304]{1,0:T(8,128)(2,1)S(1)}, bf16[128,2304]{1,0:T(8,128)(2,1)S(1)}, u32[]{:S(2)}, u32[]{:S(2)}) %collective-permute-start.11) | collective-permute-done | bytes 589856 | tf_op jit(solution)/shard_map/ppermute | solution.py:394
  61.3 2.7 %collective-permute-start.13 = (f32[36,8,128]{2,1,0:T(8,128)S(1)}, f32[36,8,128]{2,1,0:T(8,128)S(1)}, u32[]{:S(2)}, u32[]{:S(2)}) collective-permute-start(f32[36,8,128]{2,1,0:T(8,128)S(1)} %add.42.mine_ref), channel_id=1, source_target_pairs={{0,4},{4,0},{1,5},{5,1},{2,6},{6,2},{3,7},{7,3},{8,12},{12,8},{9,1... | collective-permute-start | bytes 442376 | tf_op jit(solution)/shard_map/ppermute | solution.py:390
  65.0 3.7 %right_partial.1 = (f32[36,8,128]{2,1,0:T(8,128)S(1)}, f32[36,8,128]{2,1,0:T(8,128)S(1)}, f32[32,2304]{1,0:T(8,128)S(1)}) custom-call(s32[1]{0:T(128)} %bitcast.core_ref, f32[36,8,128]{2,1,0:T(8,128)S(1)} %add.42.mine_ref, f32[36,8,128]{2,1,0:T(8,128)S(1)} %collective-permute-done.13.other_ref, bf16[2304,1024]{1,0:T(8,128)(2,1)S(1)} %turned.5.xt_ref, ...), custom_call_target="tpu_custom_call" | custom-call | flops 5133828096 | tf_op jit(solution)/shard_map/right_partial/pallas_call | solution.py:51
  71.6 4.1 %factor.1 = (f32[32,2304]{1,0:T(8,128)S(1)}, bf16[2304,192]{1,0:T(8,128)(2,1)S(1)}, bf16[32,192]{1,0:T(8,128)(2,1)S(1)}) custom-call(f32[32,2304]{1,0:T(8,128)S(1)} %get-tuple-element.78.p_ref), custom_call_target="tpu_custom_call" | custom-call | flops 4000000000 | tf_op jit(solution)/shard_map/factor/pallas_call | solution.py:51
  75.8 2.3 %collective-permute-start.16 = (f32[36,8,128]{2,1,0:T(8,128)S(1)}, f32[36,8,128]{2,1,0:T(8,128)S(1)}, u32[]{:S(2)}, u32[]{:S(2)}) collective-permute-start(f32[36,8,128]{2,1,0:T(8,128)S(1)} %add.44), channel_id=1, source_target_pairs={{32,64},{96,0},{64,32},{0,96},{33,65},{97,1},{65,33},{1,97},{34,66... | collective-permute-start | bytes 442376 | tf_op jit(solution)/shard_map/ppermute | solution.py:390
  78.0 3.8 %combined.3.refs_0_ = f32[768,2304]{1,0:T(8,128)S(1)} custom-call(bf16[2304,1024]{1,0:T(8,128)(2,1)S(1)} %turned.5.xt_ref, bf16[1024,2304]{1,0:T(8,128)(2,1)S(1)} %loaded.3.g_ref, bf16[2304,2304]{1,0:T(8,128)(2,1)S(1)} %loaded.2.e_ref), custom_call_target="tpu_custom_call" | custom-call | flops 3623878656 | tf_op jit(solution)/shard_map/combined/pallas_call | solution.py:51
  83.3 3.8 %combined.4.refs_1_ = f32[768,2304]{1,0:T(8,128)S(1)} custom-call(bf16[2304,1024]{1,0:T(8,128)(2,1)S(1)} %turned.5.xt_ref, bf16[1024,2304]{1,0:T(8,128)(2,1)S(1)} %loaded.3.g_ref, bf16[2304,2304]{1,0:T(8,128)(2,1)S(1)} %loaded.2.e_ref), custom_call_target="tpu_custom_call" | custom-call | flops 3623878656 | tf_op jit(solution)/shard_map/combined/pallas_call | solution.py:51
  87.2 2.0 %collective-permute-start.18 = (f32[36,8,128]{2,1,0:T(8,128)S(1)}, f32[36,8,128]{2,1,0:T(8,128)S(1)}, u32[]{:S(2)}, u32[]{:S(2)}) collective-permute-start(f32[36,8,128]{2,1,0:T(8,128)S(1)} %add.46), channel_id=1, source_target_pairs={{8,16},{24,0},{16,8},{0,24},{9,17},{25,1},{17,9},{1,25},{10,18},{2... | collective-permute-start | bytes 442376 | tf_op jit(solution)/shard_map/ppermute | solution.py:390
  89.2 3.8 %combined.5.refs_2_ = f32[768,2304]{1,0:T(8,128)S(1)} custom-call(bf16[2304,1024]{1,0:T(8,128)(2,1)S(1)} %turned.5.xt_ref, bf16[1024,2304]{1,0:T(8,128)(2,1)S(1)} %loaded.3.g_ref, bf16[2304,2304]{1,0:T(8,128)(2,1)S(1)} %loaded.2.e_ref), custom_call_target="tpu_custom_call" | custom-call | flops 3623878656 | tf_op jit(solution)/shard_map/combined/pallas_call | solution.py:51
  93.0 2.7 %collective-permute-start.19 = (f32[36,8,128]{2,1,0:T(8,128)S(1)}, f32[36,8,128]{2,1,0:T(8,128)S(1)}, u32[]{:S(2)}, u32[]{:S(2)}) collective-permute-start(f32[36,8,128]{2,1,0:T(8,128)S(1)} %add.47.mine_ref), channel_id=1, source_target_pairs={{0,4},{4,0},{1,5},{5,1},{2,6},{6,2},{3,7},{7,3},{8,12},{12,8},{9,1... | collective-permute-start | bytes 442376 | tf_op jit(solution)/shard_map/ppermute | solution.py:390
  96.7 6.1 %residual.1 = (bf16[1,2304,2304]{2,1,0:T(8,128)(2,1)}, f32[32,2304]{1,0:T(8,128)}) custom-call(s32[1]{0:T(128)} %bitcast.core_ref, f32[36,8,128]{2,1,0:T(8,128)S(1)} %add.47.mine_ref, f32[36,8,128]{2,1,0:T(8,128)S(1)} %collective-permute-done.19.other_ref, bf16[32,192]{1,0:T(8,128)(2,1)S(1)} %get-tuple-element.93.inv_ref, ...), custom_call_target="tpu_custom_call" | custom-call | flops 2717908992 | bytes 10616832 | tf_op jit(solution)/shard_map/residual/pallas_call | solution.py:51
  (47 shorter events, 18.7 us)
Async XLA Ops:
  5.0 15.4 %all-to-all-start = ((f32[4,32,256]{2,1,0:T(8,128)}), f32[4,32,256]{2,1,0:T(8,128)S(1)}, u32[]{:S(2)}, u32[]{:S(2)}) async-start(f32[4,32,256]{2,1,0:T(8,128)} %get-tuple-element.50), calls=%async_computation | async-start | bytes 262144 | tf_op jit(solution)/shard_map/all_to_all | solution.py:416
  10.9 23.9 %collective-permute-start.3 = (bf16[128,2304]{1,0:T(8,128)(2,1)S(1)}, bf16[128,2304]{1,0:T(8,128)(2,1)S(1)}, u32[]{:S(2)}, u32[]{:S(2)}) collective-permute-start(bf16[128,2304]{1,0:T(8,128)(2,1)S(1)} %get-tuple-element.63), channel_id=1, source_target_pairs={{0,1},{1,2},{2,3},{3,0},{4,5},{5,6},{6,7},{7,4},{8,9},{9,10},{10,1... | collective-permute-start | bytes 1769480 | tf_op jit(solution)/shard_map/ppermute | solution.py:394
  12.4 22.4 %collective-permute-start.4 = (bf16[128,2304]{1,0:T(8,128)(2,1)}, bf16[128,2304]{1,0:T(8,128)(2,1)S(1)}, u32[]{:S(2)}, u32[]{:S(2)}) collective-permute-start(bf16[128,2304]{1,0:T(8,128)(2,1)} %get-tuple-element.62), channel_id=1, source_target_pairs={{0,3},{1,0},{2,1},{3,2},{4,7},{5,4},{6,5},{7,6},{8,11},{9,8},{10,9... | collective-permute-start | bytes 1769480 | tf_op jit(solution)/shard_map/ppermute | solution.py:394
  13.6 6.9 %copy-start = (bf16[1,256,2304]{2,1,0:T(8,128)(2,1)S(1)}, bf16[1,256,2304]{2,1,0:T(8,128)(2,1)}, u32[]{:S(2)}) copy-start(bf16[1,256,2304]{2,1,0:T(8,128)(2,1)} %param.4) | copy-start | bytes 3538948
  21.5 2.7 %collective-permute-start = (f32[36,8,128]{2,1,0:T(8,128)}, f32[36,8,128]{2,1,0:T(8,128)S(1)}, u32[]{:S(2)}, u32[]{:S(2)}) collective-permute-start(f32[36,8,128]{2,1,0:T(8,128)} %get-tuple-element.53), channel_id=1, source_target_pairs={{0,4},{4,0},{1,5},{5,1},{2,6},{6,2},{3,7},{7,3},{8,12},{12,8},{9,1... | collective-permute-start | bytes 442376 | tf_op jit(solution)/shard_map/ppermute | solution.py:390
  24.3 6.1 %collective-permute-start.1 = (f32[36,8,128]{2,1,0:T(8,128)S(1)}, f32[36,8,128]{2,1,0:T(8,128)S(1)}, u32[]{:S(2)}, u32[]{:S(2)}) collective-permute-start(f32[36,8,128]{2,1,0:T(8,128)S(1)} %add.36), channel_id=1, source_target_pairs={{0,1},{2,3},{1,0},{3,2},{4,5},{6,7},{5,4},{7,6},{8,9},{10,11},{9,8... | collective-permute-start | bytes 442376 | tf_op jit(solution)/shard_map/ppermute | solution.py:390
  30.4 5.3 %collective-permute-start.2 = (f32[36,8,128]{2,1,0:T(8,128)S(1)}, f32[36,8,128]{2,1,0:T(8,128)S(1)}, u32[]{:S(2)}, u32[]{:S(2)}) collective-permute-start(f32[36,8,128]{2,1,0:T(8,128)S(1)} %add.37), channel_id=1, source_target_pairs={{1,2},{3,0},{2,1},{0,3},{5,6},{7,4},{6,5},{4,7},{9,10},{11,8},{10,... | collective-permute-start | bytes 442376 | tf_op jit(solution)/shard_map/ppermute | solution.py:390
  32.1 16.4 %collective-permute-start.8 = (bf16[128,2304]{1,0:T(8,128)(2,1)}, bf16[128,2304]{1,0:T(8,128)(2,1)S(1)}, u32[]{:S(2)}, u32[]{:S(2)}) collective-permute-start(bf16[128,2304]{1,0:T(8,128)(2,1)} %get-tuple-element.62), channel_id=1, source_target_pairs={{0,1},{1,2},{2,3},{3,0},{4,5},{5,6},{6,7},{7,4},{8,9},{9,10},{10,1... | collective-permute-start | bytes 1769480 | tf_op jit(solution)/shard_map/ppermute | solution.py:394
  32.5 16.0 %collective-permute-start.9 = (bf16[128,2304]{1,0:T(8,128)(2,1)S(1)}, bf16[128,2304]{1,0:T(8,128)(2,1)S(1)}, u32[]{:S(2)}, u32[]{:S(2)}) collective-permute-start(bf16[128,2304]{1,0:T(8,128)(2,1)S(1)} %get-tuple-element.63), channel_id=1, source_target_pairs={{0,3},{1,0},{2,1},{3,2},{4,7},{5,4},{6,5},{7,6},{8,11},{9,8},{10,9... | collective-permute-start | bytes 1769480 | tf_op jit(solution)/shard_map/ppermute | solution.py:394
  35.7 4.4 %collective-permute-start.5 = (f32[36,8,128]{2,1,0:T(8,128)S(1)}, f32[36,8,128]{2,1,0:T(8,128)S(1)}, u32[]{:S(2)}, u32[]{:S(2)}) collective-permute-start(f32[36,8,128]{2,1,0:T(8,128)S(1)} %add.38), channel_id=1, source_target_pairs={{0,32},{64,96},{32,0},{96,64},{1,33},{65,97},{33,1},{97,65},{2,34}... | collective-permute-start | bytes 442376 | tf_op jit(solution)/shard_map/ppermute | solution.py:390
  40.1 5.6 %collective-permute-start.6 = (f32[36,8,128]{2,1,0:T(8,128)S(1)}, f32[36,8,128]{2,1,0:T(8,128)S(1)}, u32[]{:S(2)}, u32[]{:S(2)}) collective-permute-start(f32[36,8,128]{2,1,0:T(8,128)S(1)} %add.39), channel_id=1, source_target_pairs={{32,64},{96,0},{64,32},{0,96},{33,65},{97,1},{65,33},{1,97},{34,66... | collective-permute-start | bytes 442376 | tf_op jit(solution)/shard_map/ppermute | solution.py:390
  42.6 18.2 %collective-permute-start.11 = (bf16[128,2304]{1,0:T(8,128)(2,1)S(1)}, bf16[128,2304]{1,0:T(8,128)(2,1)S(1)}, u32[]{:S(2)}, u32[]{:S(2)}) collective-permute-start(bf16[128,2304]{1,0:T(8,128)(2,1)S(1)} %collective-permute-done.3.refs_1_), channel_id=1, source_target_pairs={{0,1},{1,2},{2,3},{3,0},{4,5},{5,6},{6,7},{7,4},{8,9},{9,10},{10,1... | collective-permute-start | bytes 1769480 | tf_op jit(solution)/shard_map/ppermute | solution.py:394
  42.6 18.2 %collective-permute-start.12 = (bf16[128,2304]{1,0:T(8,128)(2,1)S(1)}, bf16[128,2304]{1,0:T(8,128)(2,1)S(1)}, u32[]{:S(2)}, u32[]{:S(2)}) collective-permute-start(bf16[128,2304]{1,0:T(8,128)(2,1)S(1)} %collective-permute-done.4.refs_2_), channel_id=1, source_target_pairs={{0,3},{1,0},{2,1},{3,2},{4,7},{5,4},{6,5},{7,6},{8,11},{9,8},{10,9... | collective-permute-start | bytes 1769480 | tf_op jit(solution)/shard_map/ppermute | solution.py:394
  45.7 5.6 %collective-permute-start.7 = (f32[36,8,128]{2,1,0:T(8,128)S(1)}, f32[36,8,128]{2,1,0:T(8,128)S(1)}, u32[]{:S(2)}, u32[]{:S(2)}) collective-permute-start(f32[36,8,128]{2,1,0:T(8,128)S(1)} %add.40), channel_id=1, source_target_pairs={{0,8},{16,24},{8,0},{24,16},{1,9},{17,25},{9,1},{25,17},{2,10},{18... | collective-permute-start | bytes 442376 | tf_op jit(solution)/shard_map/ppermute | solution.py:390
  51.3 10.0 %collective-permute-start.10 = (f32[36,8,128]{2,1,0:T(8,128)S(1)}, f32[36,8,128]{2,1,0:T(8,128)S(1)}, u32[]{:S(2)}, u32[]{:S(2)}) collective-permute-start(f32[36,8,128]{2,1,0:T(8,128)S(1)} %add.41), channel_id=1, source_target_pairs={{8,16},{24,0},{16,8},{0,24},{9,17},{25,1},{17,9},{1,25},{10,18},{2... | collective-permute-start | bytes 442376 | tf_op jit(solution)/shard_map/ppermute | solution.py:390
  61.3 3.7 %collective-permute-start.13 = (f32[36,8,128]{2,1,0:T(8,128)S(1)}, f32[36,8,128]{2,1,0:T(8,128)S(1)}, u32[]{:S(2)}, u32[]{:S(2)}) collective-permute-start(f32[36,8,128]{2,1,0:T(8,128)S(1)} %add.42.mine_ref), channel_id=1, source_target_pairs={{0,4},{4,0},{1,5},{5,1},{2,6},{6,2},{3,7},{7,3},{8,12},{12,8},{9,1... | collective-permute-start | bytes 442376 | tf_op jit(solution)/shard_map/ppermute | solution.py:390
  68.7 1.5 %collective-permute-start.14 = (f32[36,8,128]{2,1,0:T(8,128)S(1)}, f32[36,8,128]{2,1,0:T(8,128)S(1)}, u32[]{:S(2)}, u32[]{:S(2)}) collective-permute-start(f32[36,8,128]{2,1,0:T(8,128)S(1)} %get-tuple-element.76), channel_id=1, source_target_pairs={{0,4},{4,0},{1,5},{5,1},{2,6},{6,2},{3,7},{7,3},{8,12},{12,8},{9,1... | collective-permute-start | bytes 442376 | tf_op jit(solution)/shard_map/ppermute | solution.py:390
  70.1 5.6 %collective-permute-start.15 = (f32[36,8,128]{2,1,0:T(8,128)S(1)}, f32[36,8,128]{2,1,0:T(8,128)S(1)}, u32[]{:S(2)}, u32[]{:S(2)}) collective-permute-start(f32[36,8,128]{2,1,0:T(8,128)S(1)} %add.43), channel_id=1, source_target_pairs={{0,32},{64,96},{32,0},{96,64},{1,33},{65,97},{33,1},{97,65},{2,34}... | collective-permute-start | bytes 442376 | tf_op jit(solution)/shard_map/ppermute | solution.py:390
  75.8 6.1 %collective-permute-start.16 = (f32[36,8,128]{2,1,0:T(8,128)S(1)}, f32[36,8,128]{2,1,0:T(8,128)S(1)}, u32[]{:S(2)}, u32[]{:S(2)}) collective-permute-start(f32[36,8,128]{2,1,0:T(8,128)S(1)} %add.44), channel_id=1, source_target_pairs={{32,64},{96,0},{64,32},{0,96},{33,65},{97,1},{65,33},{1,97},{34,66... | collective-permute-start | bytes 442376 | tf_op jit(solution)/shard_map/ppermute | solution.py:390
  81.9 5.2 %collective-permute-start.17 = (f32[36,8,128]{2,1,0:T(8,128)S(1)}, f32[36,8,128]{2,1,0:T(8,128)S(1)}, u32[]{:S(2)}, u32[]{:S(2)}) collective-permute-start(f32[36,8,128]{2,1,0:T(8,128)S(1)} %add.45), channel_id=1, source_target_pairs={{0,8},{16,24},{8,0},{24,16},{1,9},{17,25},{9,1},{25,17},{2,10},{18... | collective-permute-start | bytes 442376 | tf_op jit(solution)/shard_map/ppermute | solution.py:390
  87.2 5.8 %collective-permute-start.18 = (f32[36,8,128]{2,1,0:T(8,128)S(1)}, f32[36,8,128]{2,1,0:T(8,128)S(1)}, u32[]{:S(2)}, u32[]{:S(2)}) collective-permute-start(f32[36,8,128]{2,1,0:T(8,128)S(1)} %add.46), channel_id=1, source_target_pairs={{8,16},{24,0},{16,8},{0,24},{9,17},{25,1},{17,9},{1,25},{10,18},{2... | collective-permute-start | bytes 442376 | tf_op jit(solution)/shard_map/ppermute | solution.py:390
  93.0 3.7 %collective-permute-start.19 = (f32[36,8,128]{2,1,0:T(8,128)S(1)}, f32[36,8,128]{2,1,0:T(8,128)S(1)}, u32[]{:S(2)}, u32[]{:S(2)}) collective-permute-start(f32[36,8,128]{2,1,0:T(8,128)S(1)} %add.47.mine_ref), channel_id=1, source_target_pairs={{0,4},{4,0},{1,5},{5,1},{2,6},{6,2},{3,7},{7,3},{8,12},{12,8},{9,1... | collective-permute-start | bytes 442376 | tf_op jit(solution)/shard_map/ppermute | solution.py:390
